TPU v7x, 256 devices: a whole 4x4x8 slice. The times are simulated.
256 devices in a mesh: sweep: 4 (over x), dom: 64 (over z, y, core).
Axes of the slice: x: 4, y: 4, z: 8, core: 2. Of those that a mesh axis runs over, the one named last changes fastest.
Arguments:
- fluid_state: float32 [5, 4194304], P(None, ('sweep', 'dom')), parts along dimension 1, may hold values from -6 to 6
- residual_base: float32 [5, 4194304], P(None, ('sweep', 'dom')), parts along dimension 1, may hold values from -6 to 6
- jacobian: bfloat16 [7, 5, 5, 4194304], P(None, None, None, ('sweep', 'dom')), parts along dimension 3, may hold values from -1 to 1
- columns: int32 [7, 4194304], P(None, ('sweep', 'dom')), parts along dimension 1, may hold values from 0 to 19455, as said below
- pseudo_step: float32 [4194304], P(('sweep', 'dom')), parts along dimension 0, may hold values from 0.1 to 1
- send_cells: int32 [1536, 512], P(('sweep', 'dom')), parts along dimension 0, may hold values from 0 to 16383
- interface_face_cell: int32 [1048576], P(('sweep', 'dom')), parts along dimension 0, may hold values from 0 to 16383
- interface_face_area_vector: float32 [3, 1048576], P(None, ('sweep', 'dom')), parts along dimension 1, may hold values from -6 to 6
- mortar_weight: float32 [1048576], P(('sweep', 'dom')), parts along dimension 0, may hold values from 0.5 to 1.5
- face_route: int32 [1048576, 1], P(('sweep', 'dom')), parts along dimension 0, may hold values from 0 to 63; in each aligned block of 4096 rows (0 to 4095, 4096 to 8191, ...) at most 128 rows name the same one
- face_node: int32 [1048576], P(('sweep', 'dom')), parts along dimension 0, may hold values from 0 to 511
- compliance: float32 [1024, 384, 384], P(('sweep', 'dom')), parts along dimension 0, may hold values from -0.3125 to 0.3125
Outputs:
- residual: float32 [5, 4194304], P(None, ('sweep', 'dom')), parts along dimension 1
- displacement: float32 [3, 131072], P(None, ('sweep', 'dom')), parts along dimension 1
- face_motion: float32 [3, 1048576], P(None, ('sweep', 'dom')), parts along dimension 1
There are 4 independent parts, one for each index of `sweep`. A program takes and returns all parts, laid end to end along the dimension named above; each array names one. Nothing has to cross between parts.
Inputs may be any that keep to these rules, and one draw needn't show every extreme that they name: `columns`: a value j >= 16384 refers to halo slot j - 16384, from neighbour group n = (j - 16384) // 512, and only where the neighbour device d + o[n] of the cell's device d exists (0 <= d + o[n] < number of dom devices). For a cell at local position l with row block q = l // 512: a value j < 16384 satisfies q * 512 - 64 <= j < (q + 1) * 512 + 64, and a value j >= 16384 has q * 16 <= (j - 16384) % 512 < (q + 1) * 16. `send_cells`: row p times 6 plus m lists local cells of device p that device p + o[m] reads; rows whose device p + o[m] does not exist are read by nobody. `face_route`: among the faces of one device at most 128 name the same structure device, and in every draw some device's faces name one structure device exactly 128 times.
All inputs are finite; a program needn't handle non-finite values.
Results may differ from a plain program's by a relative error of at most 0.0003.
Values sent between devices are 32-bit elements; how exact they have to be, the bound alone decides.
A program may use at most 128 MiB of HBM per device.

v0:
```python
import jax
import jax.numpy as jnp
from jax import lax
from jax.sharding import PartitionSpec as P

OFFSETS = (-3, -2, -1, 1, 2, 3)
HIGH = lax.Precision.HIGHEST


def from_behind(block, axis, distance):
    devices = range(lax.axis_size(axis))
    route = [(i - distance, i) for i in devices if i - distance in devices]
    return lax.ppermute(block, axis, route)


def apply_blocks(jacobian, selected_entries):
    ordered = jnp.transpose(selected_entries, (1, 0, 2))[:, None, :, :]
    return jnp.sum(jacobian.astype(jnp.float32) * ordered, axis=(0, 2))


def shell_tile_response(node_load, compliance):
    tiles_here = compliance.shape[0]
    tile_nodes = compliance.shape[1] // 3
    tiles = (
        node_load.reshape(3, tiles_here, tile_nodes)
        .transpose(1, 0, 2)
        .reshape(tiles_here, 3 * tile_nodes)
    )
    moved = jnp.einsum("tij,tj->ti", compliance, tiles, precision=HIGH)
    return (
        moved.reshape(tiles_here, 3, tile_nodes)
        .transpose(1, 0, 2)
        .reshape(3, tiles_here * tile_nodes)
    )


def window_pick(fluid_state, halo, columns):
    cells = fluid_state.shape[1]
    blocks = columns.shape[0]
    neighbours = halo.shape[1] // (halo.shape[1] // len(OFFSETS))
    slot_len = halo.shape[1] // neighbours
    block_rows = min(512, cells)
    reach = block_rows // 8
    slot_width = slot_len * block_rows // cells
    block_count = cells // block_rows
    grouping = 2
    turns = block_count // grouping
    padded = jnp.pad(fluid_state, ((0, 0), (reach, reach)))
    halo_groups = halo.reshape(5, neighbours, slot_len)
    local_width = block_rows + 2 * reach

    def one_block(quarter, block_columns):
        inside = block_columns < cells
        local_pos = block_columns - quarter * block_rows + reach
        shifted = jnp.maximum(block_columns - cells, 0)
        halo_pos = shifted // slot_len * slot_width + shifted % slot_len - quarter * slot_width
        local_win = lax.dynamic_slice_in_dim(padded, quarter * block_rows, local_width, 1)
        halo_win = lax.dynamic_slice_in_dim(
            halo_groups, quarter * slot_width, slot_width, 2
        ).reshape(5, neighbours * slot_width)
        window = jnp.concatenate([local_win, halo_win], axis=1)
        where_at = jnp.where(inside, local_pos, local_width + halo_pos)
        width = window.shape[1]
        onehot = (where_at[:, :, None] == jnp.arange(width, dtype=jnp.int32)[None, None, :]).astype(
            jnp.float32
        )
        return jnp.einsum("cw,biw->cbi", window, onehot, precision=HIGH)

    block_cols = columns.reshape(blocks, turns, grouping, block_rows).transpose(1, 2, 0, 3)

    def one_turn(args):
        turn, turn_cols = args
        quarters = turn * grouping + jnp.arange(grouping, dtype=jnp.int32)
        return jax.vmap(one_block)(quarters, turn_cols)

    result = lax.map(one_turn, (jnp.arange(turns, dtype=jnp.int32), block_cols))
    return result.transpose(2, 3, 0, 1, 4).reshape(5, blocks, cells)


def per_device(
    fluid_state,
    residual_base,
    jacobian,
    columns,
    pseudo_step,
    send_cells,
    interface_face_cell,
    interface_face_area_vector,
    mortar_weight,
    face_route,
    face_node,
    compliance,
):
    peers = lax.axis_size("dom")
    tile_groups = send_cells.shape[0]
    slot_len = send_cells.shape[1]
    outgoing = fluid_state[:, send_cells.reshape(-1)]
    arrived = [None] * tile_groups
    for which in range(tile_groups):
        piece = outgoing[:, which * slot_len : (which + 1) * slot_len]
        arrived[tile_groups - 1 - which] = from_behind(piece, "dom", OFFSETS[which])
    halo = jnp.concatenate(arrived, axis=1)
    coupled_system = apply_blocks(jacobian, window_pick(fluid_state, halo, columns))
    residual = residual_base - coupled_system
    cell_state = fluid_state + pseudo_step[None, :] * residual
    cell_pressure = 0.4 * (cell_state[4] - 0.8 * cell_state[1] + 0.32 * cell_state[0])
    pressure = cell_pressure[interface_face_cell]
    load = (mortar_weight * pressure)[None, :] * interface_face_area_vector
    route = face_route[:, 0]
    nodes_here = compliance.shape[0] * (compliance.shape[1] // 3)
    faces_here = interface_face_cell.shape[0]
    route_onehot = (route[:, None] == jnp.arange(peers, dtype=jnp.int32)[None, :]).astype(
        jnp.float32
    )
    spread_load = (load.T[:, :, None] * route_onehot[:, None, :]).reshape(faces_here, 3 * peers)
    capacity = 2 * faces_here // peers
    face_block = min(512, faces_here)
    face_blocks = faces_here // face_block
    blocked = route_onehot.reshape(face_blocks, face_block, peers)
    lower = (jnp.arange(face_block)[:, None] >= jnp.arange(face_block)[None, :]).astype(jnp.float32)
    inner = jnp.einsum("ij,bjp->bip", lower, blocked, precision=HIGH)
    earlier = (jnp.arange(face_blocks)[:, None] > jnp.arange(face_blocks)[None, :]).astype(
        jnp.float32
    )
    before = jnp.einsum("ab,bp->ap", earlier, jnp.sum(blocked, axis=1), precision=HIGH)
    running = inner + before[:, None, :]
    rank = jnp.sum(blocked * running, axis=2).reshape(faces_here) - 1.0
    rank_onehot = (rank[:, None] == jnp.arange(capacity, dtype=jnp.float32)[None, :]).astype(
        jnp.float32
    )
    sent_loads = jnp.einsum("fa,fk->ak", spread_load, rank_onehot, precision=HIGH).reshape(
        3, peers * capacity
    )
    node_spread = face_node.astype(jnp.float32)[:, None] * route_onehot
    sent_nodes = (
        jnp.einsum("fp,fk->pk", node_spread, rank_onehot, precision=HIGH)
        .reshape(1, peers * capacity)
        .astype(jnp.int32)
    )
    got_loads, got_nodes = (
        lax.all_to_all(sent_loads, "dom", split_axis=1, concat_axis=1, tiled=True),
        lax.all_to_all(sent_nodes, "dom", split_axis=1, concat_axis=1, tiled=True),
    )
    got_onehot = (got_nodes[0][:, None] == jnp.arange(nodes_here, dtype=jnp.int32)[None, :]).astype(
        jnp.float32
    )
    node_load = jnp.dot(got_loads, got_onehot, precision=HIGH)
    displacement = shell_tile_response(node_load, compliance)
    reply = jnp.dot(displacement, got_onehot.T, precision=HIGH)
    returned = lax.all_to_all(reply, "dom", split_axis=1, concat_axis=1, tiled=True)
    per_face = jnp.einsum(
        "fk,cpk->fcp", rank_onehot, returned.reshape(3, peers, capacity), precision=HIGH
    )
    face_motion = mortar_weight[None, :] * jnp.sum(per_face * route_onehot[:, None, :], axis=2).T
    return (residual, displacement, face_motion)


def solution(mesh):
    return jax.shard_map(
        per_device,
        mesh=mesh,
        in_specs=(
            P(None, ("sweep", "dom")),
            P(None, ("sweep", "dom")),
            P(None, None, None, ("sweep", "dom")),
            P(None, ("sweep", "dom")),
            P(("sweep", "dom")),
            P(("sweep", "dom"), None),
            P(("sweep", "dom")),
            P(None, ("sweep", "dom")),
            P(("sweep", "dom")),
            P(("sweep", "dom"), None),
            P(("sweep", "dom")),
            P(("sweep", "dom"), None, None),
        ),
        out_specs=(P(None, ("sweep", "dom")), P(None, ("sweep", "dom")), P(None, ("sweep", "dom"))),
        check_vma=False,
    )
```

profile of v0, /device:TPU:1, one launch (start us, length us, event | category | flops | bytes accessed | tf_op | source)
XLA Modules:
  0.0 468.9 jit_solution(14801468207124221326)
XLA Ops:
  0.7 5.9 %copy.25 = f32[5,16384]{0,1:T(8,128)} copy(f32[5,16384]{1,0:T(8,128)} %param.14) | data formatting | bytes 655360 | tf_op args[0]
  6.6 14.2 %gather_fusion.1 = f32[3072,5]{1,0:T(8,128)} fusion(f32[5,16384]{0,1:T(8,128)} %copy.25, s32[3072]{0:T(1024)S(1)} %broadcast_clamp_fusion), kind=kCustom, calls=%fused_computation.1 | custom fusion | bytes 135168 | tf_op jit(solution)/shard_map/gather | solution.py:97
  23.4 6.9 %collective-permute-start = (f32[5,512]{0,1:T(8,128)}, f32[5,512]{0,1:T(8,128)}, u32[]{:S(2)}, u32[]{:S(2)}) collective-permute-start(f32[5,512]{0,1:T(8,128)} %get-tuple-element.142), channel_id=1, source_target_pairs={{0,3},{1,4},{2,5},{3,6},{4,7},{5,8},{6,9},{7,10},{8,11},{9,12},{10... | collective-permute-start | bytes 30728 | tf_op jit(solution)/shard_map/ppermute | solution.py:13
  34.5 3.1 collective-permute-start.3
  42.8 14.2 %all-to-all-start.1 = ((s32[1,64,128]{2,0,1:T(1,128)}), s32[1,64,128]{2,0,1:T(1,128)}, u32[]{:S(2)}, u32[]{:S(2)}) async-start(s32[1,64,128]{2,0,1:T(1,128)} %bitcast.23), calls=%async_computation.1 | async-start | bytes 65536 | tf_op jit(solution)/shard_map/all_to_all | solution.py:142
  73.2 270.1 %while.15 = (s32[]{:T(128)}, f32[16,2,5,7,512]{4,2,3,1,0:T(8,128)}, s32[16]{0:T(128)S(1)}, f32[5,16512]{1,0:T(8,128)S(1)}, f32[5,6,512]{1,0,2:T(8,128)}, /*index...) while((s32[]{:T(128)}, f32[16,2,5,7,512]{4,2,3,1,0:T(8,128)}, ...), condition=%wide.region_1.2_spmd, body=%wide.region_0.1_spmd.sunk | while | flops 321979616 | bytes 3173586 | solution.py:76
  76.1 2.7 while.16
  81.9 8.1 %fusion.81 = f32[16,2,5,7,512]{4,2,3,1,0:T(8,128)} fusion(f32[16,2,5,7,512]{4,2,3,1,0:T(8,128)} %get-tuple-element.252, s32[]{:T(128)} %get-tuple-element.251, s32[2,7,512]{2,1,0:T(8,128)} %fusion.80, f32[2,5,96]{2,1,0:T(8,128)S(1)} %reshape.343, f32[2,5,640]{2,1,0:T(8,128)} %copy-done.15), kind=kOutput, calls=%fused_computation.9.clone.1 | convolution fusion | flops 321821888 | bytes 307456 | tf_op jit(solution)/shard_map/while/body/eval_jaxpr/vmap(cw,biw->cbi)/dot_general | solution.py:67
  92.9 2.7 while.16
  98.8 8.1 %fusion.81 = f32[16,2,5,7,512]{4,2,3,1,0:T(8,128)} fusion(f32[16,2,5,7,512]{4,2,3,1,0:T(8,128)} %get-tuple-element.252, s32[]{:T(128)} %get-tuple-element.251, s32[2,7,512]{2,1,0:T(8,128)} %fusion.80, f32[2,5,96]{2,1,0:T(8,128)S(1)} %reshape.343, f32[2,5,640]{2,1,0:T(8,128)} %copy-done.15), kind=kOutput, calls=%fused_computation.9.clone.1 | convolution fusion | flops 321821888 | bytes 307456 | tf_op jit(solution)/shard_map/while/body/eval_jaxpr/vmap(cw,biw->cbi)/dot_general | solution.py:67
  109.8 2.7 while.16
  115.7 8.1 %fusion.81 = f32[16,2,5,7,512]{4,2,3,1,0:T(8,128)} fusion(f32[16,2,5,7,512]{4,2,3,1,0:T(8,128)} %get-tuple-element.252, s32[]{:T(128)} %get-tuple-element.251, s32[2,7,512]{2,1,0:T(8,128)} %fusion.80, f32[2,5,96]{2,1,0:T(8,128)S(1)} %reshape.343, f32[2,5,640]{2,1,0:T(8,128)} %copy-done.15), kind=kOutput, calls=%fused_computation.9.clone.1 | convolution fusion | flops 321821888 | bytes 307456 | tf_op jit(solution)/shard_map/while/body/eval_jaxpr/vmap(cw,biw->cbi)/dot_general | solution.py:67
  126.7 2.7 while.16
  132.5 8.1 %fusion.81 = f32[16,2,5,7,512]{4,2,3,1,0:T(8,128)} fusion(f32[16,2,5,7,512]{4,2,3,1,0:T(8,128)} %get-tuple-element.252, s32[]{:T(128)} %get-tuple-element.251, s32[2,7,512]{2,1,0:T(8,128)} %fusion.80, f32[2,5,96]{2,1,0:T(8,128)S(1)} %reshape.343, f32[2,5,640]{2,1,0:T(8,128)} %copy-done.15), kind=kOutput, calls=%fused_computation.9.clone.1 | convolution fusion | flops 321821888 | bytes 307456 | tf_op jit(solution)/shard_map/while/body/eval_jaxpr/vmap(cw,biw->cbi)/dot_general | solution.py:67
  143.6 2.7 while.16
  149.4 8.1 %fusion.81 = f32[16,2,5,7,512]{4,2,3,1,0:T(8,128)} fusion(f32[16,2,5,7,512]{4,2,3,1,0:T(8,128)} %get-tuple-element.252, s32[]{:T(128)} %get-tuple-element.251, s32[2,7,512]{2,1,0:T(8,128)} %fusion.80, f32[2,5,96]{2,1,0:T(8,128)S(1)} %reshape.343, f32[2,5,640]{2,1,0:T(8,128)} %copy-done.15), kind=kOutput, calls=%fused_computation.9.clone.1 | convolution fusion | flops 321821888 | bytes 307456 | tf_op jit(solution)/shard_map/while/body/eval_jaxpr/vmap(cw,biw->cbi)/dot_general | solution.py:67
  160.5 2.7 while.16
  166.3 8.1 %fusion.81 = f32[16,2,5,7,512]{4,2,3,1,0:T(8,128)} fusion(f32[16,2,5,7,512]{4,2,3,1,0:T(8,128)} %get-tuple-element.252, s32[]{:T(128)} %get-tuple-element.251, s32[2,7,512]{2,1,0:T(8,128)} %fusion.80, f32[2,5,96]{2,1,0:T(8,128)S(1)} %reshape.343, f32[2,5,640]{2,1,0:T(8,128)} %copy-done.15), kind=kOutput, calls=%fused_computation.9.clone.1 | convolution fusion | flops 321821888 | bytes 307456 | tf_op jit(solution)/shard_map/while/body/eval_jaxpr/vmap(cw,biw->cbi)/dot_general | solution.py:67
  177.3 2.7 while.16
  183.2 8.1 %fusion.81 = f32[16,2,5,7,512]{4,2,3,1,0:T(8,128)} fusion(f32[16,2,5,7,512]{4,2,3,1,0:T(8,128)} %get-tuple-element.252, s32[]{:T(128)} %get-tuple-element.251, s32[2,7,512]{2,1,0:T(8,128)} %fusion.80, f32[2,5,96]{2,1,0:T(8,128)S(1)} %reshape.343, f32[2,5,640]{2,1,0:T(8,128)} %copy-done.15), kind=kOutput, calls=%fused_computation.9.clone.1 | convolution fusion | flops 321821888 | bytes 307456 | tf_op jit(solution)/shard_map/while/body/eval_jaxpr/vmap(cw,biw->cbi)/dot_general | solution.py:67
  194.2 2.7 while.16
  200.1 8.1 %fusion.81 = f32[16,2,5,7,512]{4,2,3,1,0:T(8,128)} fusion(f32[16,2,5,7,512]{4,2,3,1,0:T(8,128)} %get-tuple-element.252, s32[]{:T(128)} %get-tuple-element.251, s32[2,7,512]{2,1,0:T(8,128)} %fusion.80, f32[2,5,96]{2,1,0:T(8,128)S(1)} %reshape.343, f32[2,5,640]{2,1,0:T(8,128)} %copy-done.15), kind=kOutput, calls=%fused_computation.9.clone.1 | convolution fusion | flops 321821888 | bytes 307456 | tf_op jit(solution)/shard_map/while/body/eval_jaxpr/vmap(cw,biw->cbi)/dot_general | solution.py:67
  211.1 2.7 while.16
  217.0 8.1 %fusion.81 = f32[16,2,5,7,512]{4,2,3,1,0:T(8,128)} fusion(f32[16,2,5,7,512]{4,2,3,1,0:T(8,128)} %get-tuple-element.252, s32[]{:T(128)} %get-tuple-element.251, s32[2,7,512]{2,1,0:T(8,128)} %fusion.80, f32[2,5,96]{2,1,0:T(8,128)S(1)} %reshape.343, f32[2,5,640]{2,1,0:T(8,128)} %copy-done.15), kind=kOutput, calls=%fused_computation.9.clone.1 | convolution fusion | flops 321821888 | bytes 307456 | tf_op jit(solution)/shard_map/while/body/eval_jaxpr/vmap(cw,biw->cbi)/dot_general | solution.py:67
  228.0 2.7 while.16
  233.8 8.1 %fusion.81 = f32[16,2,5,7,512]{4,2,3,1,0:T(8,128)} fusion(f32[16,2,5,7,512]{4,2,3,1,0:T(8,128)} %get-tuple-element.252, s32[]{:T(128)} %get-tuple-element.251, s32[2,7,512]{2,1,0:T(8,128)} %fusion.80, f32[2,5,96]{2,1,0:T(8,128)S(1)} %reshape.343, f32[2,5,640]{2,1,0:T(8,128)} %copy-done.15), kind=kOutput, calls=%fused_computation.9.clone.1 | convolution fusion | flops 321821888 | bytes 307456 | tf_op jit(solution)/shard_map/while/body/eval_jaxpr/vmap(cw,biw->cbi)/dot_general | solution.py:67
  244.9 2.7 while.16
  250.7 8.1 %fusion.81 = f32[16,2,5,7,512]{4,2,3,1,0:T(8,128)} fusion(f32[16,2,5,7,512]{4,2,3,1,0:T(8,128)} %get-tuple-element.252, s32[]{:T(128)} %get-tuple-element.251, s32[2,7,512]{2,1,0:T(8,128)} %fusion.80, f32[2,5,96]{2,1,0:T(8,128)S(1)} %reshape.343, f32[2,5,640]{2,1,0:T(8,128)} %copy-done.15), kind=kOutput, calls=%fused_computation.9.clone.1 | convolution fusion | flops 321821888 | bytes 307456 | tf_op jit(solution)/shard_map/while/body/eval_jaxpr/vmap(cw,biw->cbi)/dot_general | solution.py:67
  261.7 2.7 while.16
  267.6 8.1 %fusion.81 = f32[16,2,5,7,512]{4,2,3,1,0:T(8,128)} fusion(f32[16,2,5,7,512]{4,2,3,1,0:T(8,128)} %get-tuple-element.252, s32[]{:T(128)} %get-tuple-element.251, s32[2,7,512]{2,1,0:T(8,128)} %fusion.80, f32[2,5,96]{2,1,0:T(8,128)S(1)} %reshape.343, f32[2,5,640]{2,1,0:T(8,128)} %copy-done.15), kind=kOutput, calls=%fused_computation.9.clone.1 | convolution fusion | flops 321821888 | bytes 307456 | tf_op jit(solution)/shard_map/while/body/eval_jaxpr/vmap(cw,biw->cbi)/dot_general | solution.py:67
  278.6 2.7 while.16
  284.5 8.1 %fusion.81 = f32[16,2,5,7,512]{4,2,3,1,0:T(8,128)} fusion(f32[16,2,5,7,512]{4,2,3,1,0:T(8,128)} %get-tuple-element.252, s32[]{:T(128)} %get-tuple-element.251, s32[2,7,512]{2,1,0:T(8,128)} %fusion.80, f32[2,5,96]{2,1,0:T(8,128)S(1)} %reshape.343, f32[2,5,640]{2,1,0:T(8,128)} %copy-done.15), kind=kOutput, calls=%fused_computation.9.clone.1 | convolution fusion | flops 321821888 | bytes 307456 | tf_op jit(solution)/shard_map/while/body/eval_jaxpr/vmap(cw,biw->cbi)/dot_general | solution.py:67
  295.5 2.7 while.16
  301.4 8.1 %fusion.81 = f32[16,2,5,7,512]{4,2,3,1,0:T(8,128)} fusion(f32[16,2,5,7,512]{4,2,3,1,0:T(8,128)} %get-tuple-element.252, s32[]{:T(128)} %get-tuple-element.251, s32[2,7,512]{2,1,0:T(8,128)} %fusion.80, f32[2,5,96]{2,1,0:T(8,128)S(1)} %reshape.343, f32[2,5,640]{2,1,0:T(8,128)} %copy-done.15), kind=kOutput, calls=%fused_computation.9.clone.1 | convolution fusion | flops 321821888 | bytes 307456 | tf_op jit(solution)/shard_map/while/body/eval_jaxpr/vmap(cw,biw->cbi)/dot_general | solution.py:67
  318.3 8.1 %fusion.81 = f32[16,2,5,7,512]{4,2,3,1,0:T(8,128)} fusion(f32[16,2,5,7,512]{4,2,3,1,0:T(8,128)} %get-tuple-element.252, s32[]{:T(128)} %get-tuple-element.251, s32[2,7,512]{2,1,0:T(8,128)} %fusion.80, f32[2,5,96]{2,1,0:T(8,128)S(1)} %reshape.343, f32[2,5,640]{2,1,0:T(8,128)} %copy-done.15), kind=kOutput, calls=%fused_computation.9.clone.1 | convolution fusion | flops 321821888 | bytes 307456 | tf_op jit(solution)/shard_map/while/body/eval_jaxpr/vmap(cw,biw->cbi)/dot_general | solution.py:67
  335.1 8.1 %fusion.81 = f32[16,2,5,7,512]{4,2,3,1,0:T(8,128)} fusion(f32[16,2,5,7,512]{4,2,3,1,0:T(8,128)} %get-tuple-element.252, s32[]{:T(128)} %get-tuple-element.251, s32[2,7,512]{2,1,0:T(8,128)} %fusion.80, f32[2,5,96]{2,1,0:T(8,128)S(1)} %reshape.343, f32[2,5,640]{2,1,0:T(8,128)} %copy-done.15), kind=kOutput, calls=%fused_computation.9.clone.1 | convolution fusion | flops 321821888 | bytes 307456 | tf_op jit(solution)/shard_map/while/body/eval_jaxpr/vmap(cw,biw->cbi)/dot_general | solution.py:67
  343.3 5.2 %copy.33 = f32[5,7,16,2,512]{4,3,2,1,0:T(2,128)} copy(f32[5,7,16,2,512]{4,0,1,3,2:T(8,128)} %bitcast.129) | data formatting | bytes 4587520 | tf_op jit(solution)/shard_map/transpose | solution.py:77
  348.5 4.4 reshape.271
  352.8 5.9 %multiply_reduce_fusion = f32[5,16384]{1,0:T(8,128)S(1)} fusion(bf16[7,5,5,16384]{3,0,2,1:T(8,128)(2,1)} %param.16, f32[7,5,16384]{2,0,1:T(8,128)} %bitcast.128), kind=kLoop, calls=%fused_computation.46 | loop fusion | flops 8519680 | bytes 8355840 | tf_op jit(solution)/shard_map/reduce_sum | solution.py:18
  359.9 40.8 %gather_fusion.2 = f32[4096]{0:T(1024)} fusion(f32[16384]{0:T(1024)S(1)} %bitcast.127, s32[4096]{0:T(1024)} %fusion.67), kind=kCustom, calls=%fused_computation.2 | custom fusion | bytes 49152 | tf_op jit(solution)/shard_map/gather | solution.py:107
  401.5 2.7 fusion.32
  404.9 13.5 %all-to-all-start = ((f32[3,64,128]{2,0,1:T(4,128)}), f32[3,64,128]{2,0,1:T(4,128)}, u32[]{:S(2)}, u32[]{:S(2)}) async-start(f32[3,64,128]{2,0,1:T(4,128)} %copy.34), calls=%async_computation | async-start | bytes 262144 | tf_op jit(solution)/shard_map/all_to_all | solution.py:141
  418.4 11.0 %all-to-all-done = f32[3,64,128]{2,0,1:T(4,128)} async-done(((f32[3,64,128]{2,0,1:T(4,128)}), f32[3,64,128]{2,0,1:T(4,128)}, u32[]{:S(2)}, u32[]{:S(2)}) %all-to-all-start) | async-done | bytes 98336 | tf_op jit(solution)/shard_map/all_to_all | solution.py:141
  429.4 7.9 %fusion.48 = f32[4,3,128]{2,1,0:T(4,128)S(1)} fusion(s32[4,128]{1,0:T(4,128)S(1)} %multiply_add_fusion.1, s32[8192]{0:T(1024)} %bitcast.24, f32[3,64,128]{2,0,1:T(4,128)} %all-to-all-done), kind=kOutput, calls=%fused_computation.65 | convolution fusion | flops 155189248 | bytes 139264 | tf_op jit(solution)/shard_map/dot_general | solution.py:147
  439.5 9.2 %fusion.25 = f32[3,64,128]{2,0,1:T(4,128)} fusion(f32[3,512,1]{1,0,2:T(4,128)S(1)} %reshape.323, s32[64,128]{1,0:T(8,128)} %bitcast.29), kind=kOutput, calls=%fused_computation.43 | convolution fusion | flops 155189248 | bytes 137216 | tf_op jit(solution)/shard_map/dot_general | solution.py:149
  448.8 5.2 %all-to-all-start.2 = ((f32[3,64,128]{2,0,1:T(4,128)}), f32[3,64,128]{2,0,1:T(4,128)}, u32[]{:S(2)}, u32[]{:S(2)}) async-start(f32[3,64,128]{2,0,1:T(4,128)} %fusion.25), calls=%async_computation.2 | async-start | bytes 262144 | tf_op jit(solution)/shard_map/all_to_all | solution.py:150
  454.6 10.7 %all-to-all-done.2 = f32[3,64,128]{2,0,1:T(4,128)} async-done(((f32[3,64,128]{2,0,1:T(4,128)}), f32[3,64,128]{2,0,1:T(4,128)}, u32[]{:S(2)}, u32[]{:S(2)}) %all-to-all-start.2) | async-done | bytes 98336 | tf_op jit(solution)/shard_map/all_to_all | solution.py:150
  465.2 3.0 fusion.41
  (420 shorter events, 168.6 us)
Async XLA Ops:
  0.6 436.7 %copy-start = (f32[4,384,384]{2,1,0:T(8,128)S(1)}, f32[4,384,384]{2,1,0:T(8,128)}, u32[]{:S(2)}) copy-start(f32[4,384,384]{2,1,0:T(8,128)} %param.25) | copy-start | bytes 7077892
  0.6 5.9 %copy-start.10 = (s32[6,512]{1,0:T(8,128)S(1)}, s32[6,512]{1,0:T(8,128)}, u32[]{:S(2)}) copy-start(s32[6,512]{1,0:T(8,128)} %param.19) | copy-start | bytes 36868
  6.5 32.9 %copy-start.6 = (s32[4096,1]{0,1:T(1,128)S(1)}, s32[4096,1]{0,1:T(1,128)}, u32[]{:S(2)}) copy-start(s32[4096,1]{0,1:T(1,128)} %param.23) | copy-start | bytes 49156
  6.5 34.5 %copy-start.11 = (s32[4096]{0:T(1024)S(1)}, s32[4096]{0:T(1024)}, u32[]{:S(2)}) copy-start(s32[4096]{0:T(1024)} %param.24) | copy-start | bytes 49156
  20.8 37.2 %copy-start.12 = (s32[4096]{0:T(1024)S(1)}, s32[4096]{0:T(1024)}, u32[]{:S(2)}) copy-start(s32[4096]{0:T(1024)} %param.20) | copy-start | bytes 49156
  20.8 37.8 %copy-start.1 = (f32[5,16384]{1,0:T(8,128)S(1)}, f32[5,16384]{1,0:T(8,128)}, u32[]{:S(2)}) copy-start(f32[5,16384]{1,0:T(8,128)} %param.14) | copy-start | bytes 983044
  23.4 35.5 %collective-permute-start = (f32[5,512]{0,1:T(8,128)}, f32[5,512]{0,1:T(8,128)}, u32[]{:S(2)}, u32[]{:S(2)}) collective-permute-start(f32[5,512]{0,1:T(8,128)} %get-tuple-element.142), channel_id=1, source_target_pairs={{0,3},{1,4},{2,5},{3,6},{4,7},{5,8},{6,9},{7,10},{8,11},{9,12},{10... | collective-permute-start | bytes 30728 | tf_op jit(solution)/shard_map/ppermute | solution.py:13
  30.3 31.5 %collective-permute-start.1 = (f32[5,512]{0,1:T(8,128)}, f32[5,512]{0,1:T(8,128)}, u32[]{:S(2)}, u32[]{:S(2)}) collective-permute-start(f32[5,512]{0,1:T(8,128)} %get-tuple-element.141), channel_id=1, source_target_pairs={{0,2},{1,3},{2,4},{3,5},{4,6},{5,7},{6,8},{7,9},{8,10},{9,11},{10,... | collective-permute-start | bytes 30728 | tf_op jit(solution)/shard_map/ppermute | solution.py:13
  32.6 30.9 %collective-permute-start.2 = (f32[5,512]{0,1:T(8,128)}, f32[5,512]{0,1:T(8,128)}, u32[]{:S(2)}, u32[]{:S(2)}) collective-permute-start(f32[5,512]{0,1:T(8,128)} %get-tuple-element.140), channel_id=1, source_target_pairs={{0,1},{1,2},{2,3},{3,4},{4,5},{5,6},{6,7},{7,8},{8,9},{9,10},{10,1... | collective-permute-start | bytes 30728 | tf_op jit(solution)/shard_map/ppermute | solution.py:13
  34.5 30.7 %collective-permute-start.3 = (f32[5,512]{0,1:T(8,128)}, f32[5,512]{0,1:T(8,128)}, u32[]{:S(2)}, u32[]{:S(2)}) collective-permute-start(f32[5,512]{0,1:T(8,128)} %get-tuple-element.139), channel_id=1, source_target_pairs={{1,0},{2,1},{3,2},{4,3},{5,4},{6,5},{7,6},{8,7},{9,8},{10,9},{11,1... | collective-permute-start | bytes 30728 | tf_op jit(solution)/shard_map/ppermute | solution.py:13
  37.6 29.2 %collective-permute-start.4 = (f32[5,512]{0,1:T(8,128)}, f32[5,512]{0,1:T(8,128)}, u32[]{:S(2)}, u32[]{:S(2)}) collective-permute-start(f32[5,512]{0,1:T(8,128)} %get-tuple-element.138), channel_id=1, source_target_pairs={{2,0},{3,1},{4,2},{5,3},{6,4},{7,5},{8,6},{9,7},{10,8},{11,9},{12,... | collective-permute-start | bytes 30728 | tf_op jit(solution)/shard_map/ppermute | solution.py:13
  41.1 28.6 %copy-start.13 = (f32[1,4,8,128]{3,1,2,0:T(4,128)}, f32[1,4,8,128]{3,1,2,0:T(4,128)S(1)}, u32[]{:S(2)}) copy-start(f32[1,4,8,128]{3,1,2,0:T(4,128)S(1)} %copy.43) | copy-start | bytes 49156
  42.8 362.1 %all-to-all-start.1 = ((s32[1,64,128]{2,0,1:T(1,128)}), s32[1,64,128]{2,0,1:T(1,128)}, u32[]{:S(2)}, u32[]{:S(2)}) async-start(s32[1,64,128]{2,0,1:T(1,128)} %bitcast.23), calls=%async_computation.1 | async-start | bytes 65536 | tf_op jit(solution)/shard_map/all_to_all | solution.py:142
  58.9 9.7 %collective-permute-start.5 = (f32[5,512]{0,1:T(8,128)}, f32[5,512]{0,1:T(8,128)}, u32[]{:S(2)}, u32[]{:S(2)}) collective-permute-start(f32[5,512]{0,1:T(8,128)} %get-tuple-element.137), channel_id=1, source_target_pairs={{3,0},{4,1},{5,2},{6,3},{7,4},{8,5},{9,6},{10,7},{11,8},{12,9},{13... | collective-permute-start | bytes 30728 | tf_op jit(solution)/shard_map/ppermute | solution.py:13
  78.7 0.8 copy-start.2
  81.9 8.1 %copy-start.3 = (f32[5,16512]{1,0:T(8,128)S(1)}, f32[5,16512]{1,0:T(8,128)}, u32[]{:S(2)}) copy-start(f32[5,16512]{1,0:T(8,128)} %copy-done.2) | copy-start | bytes 990724 | tf_op jit(solution)/shard_map/while
  95.6 0.8 copy-start.2
  98.8 8.1 %copy-start.3 = (f32[5,16512]{1,0:T(8,128)S(1)}, f32[5,16512]{1,0:T(8,128)}, u32[]{:S(2)}) copy-start(f32[5,16512]{1,0:T(8,128)} %copy-done.2) | copy-start | bytes 990724 | tf_op jit(solution)/shard_map/while
  112.5 0.8 copy-start.2
  115.7 8.1 %copy-start.3 = (f32[5,16512]{1,0:T(8,128)S(1)}, f32[5,16512]{1,0:T(8,128)}, u32[]{:S(2)}) copy-start(f32[5,16512]{1,0:T(8,128)} %copy-done.2) | copy-start | bytes 990724 | tf_op jit(solution)/shard_map/while
  129.3 0.8 copy-start.2
  132.5 8.1 %copy-start.3 = (f32[5,16512]{1,0:T(8,128)S(1)}, f32[5,16512]{1,0:T(8,128)}, u32[]{:S(2)}) copy-start(f32[5,16512]{1,0:T(8,128)} %copy-done.2) | copy-start | bytes 990724 | tf_op jit(solution)/shard_map/while
  146.2 0.8 copy-start.2
  149.4 8.1 %copy-start.3 = (f32[5,16512]{1,0:T(8,128)S(1)}, f32[5,16512]{1,0:T(8,128)}, u32[]{:S(2)}) copy-start(f32[5,16512]{1,0:T(8,128)} %copy-done.2) | copy-start | bytes 990724 | tf_op jit(solution)/shard_map/while
  163.1 0.8 copy-start.2
  166.3 8.1 %copy-start.3 = (f32[5,16512]{1,0:T(8,128)S(1)}, f32[5,16512]{1,0:T(8,128)}, u32[]{:S(2)}) copy-start(f32[5,16512]{1,0:T(8,128)} %copy-done.2) | copy-start | bytes 990724 | tf_op jit(solution)/shard_map/while
  180.0 0.8 copy-start.2
  183.2 8.1 %copy-start.3 = (f32[5,16512]{1,0:T(8,128)S(1)}, f32[5,16512]{1,0:T(8,128)}, u32[]{:S(2)}) copy-start(f32[5,16512]{1,0:T(8,128)} %copy-done.2) | copy-start | bytes 990724 | tf_op jit(solution)/shard_map/while
  196.9 0.8 copy-start.2
  200.1 8.1 %copy-start.3 = (f32[5,16512]{1,0:T(8,128)S(1)}, f32[5,16512]{1,0:T(8,128)}, u32[]{:S(2)}) copy-start(f32[5,16512]{1,0:T(8,128)} %copy-done.2) | copy-start | bytes 990724 | tf_op jit(solution)/shard_map/while
  216.9 8.2 %copy-start.3 = (f32[5,16512]{1,0:T(8,128)S(1)}, f32[5,16512]{1,0:T(8,128)}, u32[]{:S(2)}) copy-start(f32[5,16512]{1,0:T(8,128)} %copy-done.2) | copy-start | bytes 990724 | tf_op jit(solution)/shard_map/while
  233.8 8.1 %copy-start.3 = (f32[5,16512]{1,0:T(8,128)S(1)}, f32[5,16512]{1,0:T(8,128)}, u32[]{:S(2)}) copy-start(f32[5,16512]{1,0:T(8,128)} %copy-done.2) | copy-start | bytes 990724 | tf_op jit(solution)/shard_map/while
  247.5 0.8 copy-start.2
  250.7 8.1 %copy-start.3 = (f32[5,16512]{1,0:T(8,128)S(1)}, f32[5,16512]{1,0:T(8,128)}, u32[]{:S(2)}) copy-start(f32[5,16512]{1,0:T(8,128)} %copy-done.2) | copy-start | bytes 990724 | tf_op jit(solution)/shard_map/while
  264.4 0.8 copy-start.2
  267.6 8.1 %copy-start.3 = (f32[5,16512]{1,0:T(8,128)S(1)}, f32[5,16512]{1,0:T(8,128)}, u32[]{:S(2)}) copy-start(f32[5,16512]{1,0:T(8,128)} %copy-done.2) | copy-start | bytes 990724 | tf_op jit(solution)/shard_map/while
  284.5 8.2 %copy-start.3 = (f32[5,16512]{1,0:T(8,128)S(1)}, f32[5,16512]{1,0:T(8,128)}, u32[]{:S(2)}) copy-start(f32[5,16512]{1,0:T(8,128)} %copy-done.2) | copy-start | bytes 990724 | tf_op jit(solution)/shard_map/while
  301.4 8.1 %copy-start.3 = (f32[5,16512]{1,0:T(8,128)S(1)}, f32[5,16512]{1,0:T(8,128)}, u32[]{:S(2)}) copy-start(f32[5,16512]{1,0:T(8,128)} %copy-done.2) | copy-start | bytes 990724 | tf_op jit(solution)/shard_map/while
  318.2 8.2 %copy-start.3 = (f32[5,16512]{1,0:T(8,128)S(1)}, f32[5,16512]{1,0:T(8,128)}, u32[]{:S(2)}) copy-start(f32[5,16512]{1,0:T(8,128)} %copy-done.2) | copy-start | bytes 990724 | tf_op jit(solution)/shard_map/while
  335.1 8.1 %copy-start.3 = (f32[5,16512]{1,0:T(8,128)S(1)}, f32[5,16512]{1,0:T(8,128)}, u32[]{:S(2)}) copy-start(f32[5,16512]{1,0:T(8,128)} %copy-done.2) | copy-start | bytes 990724 | tf_op jit(solution)/shard_map/while
  352.8 5.9 %copy-start.5 = (f32[5,16384]{1,0:T(8,128)S(1)}, f32[5,16384]{1,0:T(8,128)}, u32[]{:S(2)}) copy-start(f32[5,16384]{1,0:T(8,128)} %param.15) | copy-start | bytes 983044
  352.8 5.9 %copy-start.9 = (f32[16384]{0:T(1024)S(1)}, f32[16384]{0:T(1024)}, u32[]{:S(2)}) copy-start(f32[16384]{0:T(1024)} %param.18) | copy-start | bytes 196612
  359.9 40.8 %copy-start.7 = (f32[4096]{0:T(1024)S(1)}, f32[4096]{0:T(1024)}, u32[]{:S(2)}) copy-start(f32[4096]{0:T(1024)} %param.22) | copy-start | bytes 49156
  359.9 41.6 %copy-start.8 = (f32[3,4096]{1,0:T(4,128)S(1)}, f32[3,4096]{1,0:T(4,128)}, u32[]{:S(2)}) copy-start(f32[3,4096]{1,0:T(4,128)} %param.21) | copy-start | bytes 147460
  359.9 41.6 %copy-start.4 = (f32[4096,64]{0,1:T(8,128)S(1)}, f32[4096,64]{0,1:T(8,128)}, u32[]{:S(2)}) copy-start(f32[4096,64]{0,1:T(8,128)} %fusion.55) | copy-start | bytes 3145732
  404.9 24.5 %all-to-all-start = ((f32[3,64,128]{2,0,1:T(4,128)}), f32[3,64,128]{2,0,1:T(4,128)}, u32[]{:S(2)}, u32[]{:S(2)}) async-start(f32[3,64,128]{2,0,1:T(4,128)} %copy.34), calls=%async_computation | async-start | bytes 262144 | tf_op jit(solution)/shard_map/all_to_all | solution.py:141
  437.3 28.0 %copy-start.14 = (f32[1,4,8,128]{3,1,2,0:T(4,128)S(1)}, f32[1,4,8,128]{3,1,2,0:T(4,128)}, u32[]{:S(2)}) copy-start(f32[1,4,8,128]{3,1,2,0:T(4,128)} %copy-done.13) | copy-start | bytes 49156
  448.8 16.5 %all-to-all-start.2 = ((f32[3,64,128]{2,0,1:T(4,128)}), f32[3,64,128]{2,0,1:T(4,128)}, u32[]{:S(2)}, u32[]{:S(2)}) async-start(f32[3,64,128]{2,0,1:T(4,128)} %fusion.25), calls=%async_computation.2 | async-start | bytes 262144 | tf_op jit(solution)/shard_map/all_to_all | solution.py:150
  (22 other events, 14.8 us)
where the time goes:
time: 472 us; the launch traced here: 469 us
  local copies, waits for them, and re-layouts  192 us (41%)
  matrix products  157 us (33%)
  starting transfers between devices  49.7 us (11%)
  other arithmetic  36.3 us (8%)
  waiting for transfers between devices  21.7 us (5%)
  loops' own time  11 us (2%)
    dot_general x16, matrix products, one_block(): return jnp.einsum('cw,biw->cbi', window, onehot, precision=HIGH)  130 us
    gather x96, local copies, waits for them, and re-layouts  42.4 us
    gather x1, local copies, waits for them, and re-layouts, per_device(): pressure = cell_pressure[interface_face_cell]  40.8 us
    gather x16, local copies, waits for them, and re-layouts, one_block(): lax.dynamic_slice_in_dim(halo_groups, quarter * slot_width, slot_width, 2)  34.3 us
    select_n x16, other arithmetic, one_block(): where_at = jnp.where(inside, local_pos, local_width + halo_pos)  23.3 us
    ppermute x6, starting transfers between devices, from_behind(): return lax.ppermute(block, axis, route)  16.8 us
    gather x1, local copies, waits for them, and re-layouts, per_device(): outgoing = fluid_state[:, send_cells.reshape(-1)]  14.2 us
    all_to_all x1, starting transfers between devices, per_device(): lax.all_to_all(sent_nodes, 'dom', split_axis=1, concat_axis=1, tiled=True)  14.2 us
  transfers between devices with their start and end apart: 9, of which 2 were waited for; matrix products, arithmetic and copies ran while one was open for 70% of the time, Pallas kernels for 0%

commit v1 on v0

v1 whole, which is shorter than its diff:
```python
import functools

import jax
import jax.numpy as jnp
from jax import lax
from jax.experimental import pallas as pl
from jax.experimental.pallas import tpu as pltpu
from jax.sharding import PartitionSpec as P

MESH = pl.DeviceIdType.MESH
OFFSETS = (-3, -2, -1, 1, 2, 3)
HIGH = lax.Precision.HIGHEST
F32 = jnp.float32
BF16 = jnp.bfloat16
I32 = jnp.int32
LANES = 128


def pick(row, where_at):
    return jnp.take_along_axis(
        jnp.broadcast_to(row, where_at.shape), where_at, axis=1, mode="promise_in_bounds"
    )


def iota(shape, dim):
    return lax.broadcasted_iota(I32, shape, dim)


def lanes(block):
    return pl.ds(pl.multiple_of(block * LANES, LANES), LANES)


def three_parts(value):
    high = value.astype(BF16)
    rest = value - high.astype(F32)
    middle = rest.astype(BF16)
    low = (rest - middle.astype(F32)).astype(BF16)
    return high, middle, low


def dot_nt(a, b, precision=None):
    return lax.dot_general(
        a, b, (((1,), (1,)), ((), ())), precision=precision, preferred_element_type=F32
    )


def gather_sends(fluid, send, index, out):
    index[0:6, :] = send[...]
    index[6:8, :] = jnp.zeros((2, index.shape[1]), I32)
    cells = [index[:, k * LANES : (k + 1) * LANES] for k in range(4)]
    low = [cell & (LANES - 1) for cell in cells]
    high = [cell >> 7 for cell in cells]

    def step(block, total):
        total = list(total)
        hit = [h == block for h in high]
        for c in range(5):
            row = fluid[pl.ds(c, 1), lanes(block)]
            for k in range(4):
                total[c * 4 + k] = jnp.where(hit[k], pick(row, low[k]), total[c * 4 + k])
        return tuple(total)

    total = lax.fori_loop(
        0, 128, step, tuple(jnp.zeros((8, LANES), F32) for _ in range(20)), unroll=4
    )
    for slot in range(20):
        out[pl.ds(slot, 8, stride=24), :] = total[slot]


def shift_table(fluid, table):
    left = iota((5, LANES), 1) < 64

    def step(block, before):
        here = pltpu.roll(fluid[:, lanes(block)], 64, 1)
        table[block, 0:5, :] = jnp.where(left, before, here)
        return here

    last = lax.fori_loop(0, 128, step, jnp.zeros((5, LANES), F32), unroll=4)
    table[128, 0:5, :] = last


def rank_faces(me, peers, route, relative, onehot, prefix, rank):
    relative[...] = (route[...] - me) & (peers - 1)
    line = iota((peers, LANES), 0)
    for i in range(32):
        hit = jnp.broadcast_to(relative[i : i + 1, :], (peers, LANES)) == line
        onehot[i * peers : (i + 1) * peers, :] = jnp.where(hit, 1.0, 0.0).astype(BF16)
    upto = jnp.where(iota((LANES, LANES), 0) <= iota((LANES, LANES), 1), 1.0, 0.0)
    weights = jnp.concatenate([upto, jnp.ones((LANES, LANES), F32)], axis=1).astype(BF16)

    def count(part, carry):
        rows = pl.ds(pl.multiple_of(part * 512, 512), 512)
        prefix[rows, :] = jnp.dot(onehot[rows, :], weights, preferred_element_type=F32)
        return carry

    lax.fori_loop(0, 32 * peers // 512, count, 0)

    def step(i, before):
        rows = pl.ds(pl.multiple_of(i * peers, peers), peers)
        hit = onehot[rows, :].astype(F32)
        here = prefix[rows, 0:LANES] + before
        rank[pl.ds(i, 1), :] = jnp.sum(hit * here, axis=0, keepdims=True) - 1.0
        return before + prefix[rows, LANES : 2 * LANES]

    lax.fori_loop(0, 32, step, jnp.zeros((peers, LANES), F32), unroll=2)


def compact_faces(peers, onehot, rank, fcell, fnode, weight, area, cell_at, slab, scale_at):
    line = iota((LANES, LANES), 0).astype(F32)
    lane = iota((peers, LANES), 1).astype(F32)

    def step(pair, total):
        left, right = [], []
        for half in range(2):
            i = pair * 2 + half
            hit = onehot[pl.ds(pl.multiple_of(i * peers, peers), peers), :].astype(F32)
            left.append(
                jnp.concatenate(
                    [hit * (i + 1).astype(F32), hit * lane], axis=0
                ).astype(BF16)
            )
            place = jnp.broadcast_to(rank[pl.ds(i, 1), :], (LANES, LANES)) == line
            right.append(jnp.where(place, 1.0, 0.0).astype(BF16))
        return total + dot_nt(jnp.concatenate(left, axis=1), jnp.concatenate(right, axis=1))

    found = lax.fori_loop(0, 16, step, jnp.zeros((2 * peers, LANES), F32))
    high = found[0:peers, :].astype(I32) - 1
    low = found[peers : 2 * peers, :].astype(I32)
    groups = peers // 8
    for g in range(groups):
        h = high[g * 8 : g * 8 + 8, :]
        l = low[g * 8 : g * 8 + 8, :]

        def look(i, total, h=h, l=l):
            hit = h == i
            rows = (
                fcell[pl.ds(i, 1), :],
                fnode[pl.ds(i, 1), :],
                weight[pl.ds(i, 1), :] * area[0:1, lanes(i)],
                weight[pl.ds(i, 1), :] * area[1:2, lanes(i)],
                weight[pl.ds(i, 1), :] * area[2:3, lanes(i)],
            )
            return tuple(jnp.where(hit, pick(row, l), old) for row, old in zip(rows, total))

        none_i = jnp.zeros((8, LANES), I32)
        none_f = jnp.zeros((8, LANES), F32)
        cell, node, *scales = lax.fori_loop(
            0, 32, look, (none_i, none_i, none_f, none_f, none_f), unroll=8
        )
        cell_at[g * 8 : g * 8 + 8, :] = cell
        slab[g * 8 : g * 8 + 8, 3, :] = node.astype(F32)
        for c in range(3):
            scale_at[c, g * 8 : g * 8 + 8, :] = scales[c]


def halo_table(arrived, table):
    line, lane = iota((8, LANES), 0), iota((8, LANES), 1)
    where_at = line * 16 + (lane & 15)
    for c in range(5):
        for quarter in range(4):
            total = jnp.zeros((8, LANES), F32)
            for n in range(6):
                got = pick(arrived[n, c * 4 + quarter : c * 4 + quarter + 1, :], where_at)
                total = jnp.where((lane >> 4) == n, got, total)
            table[c, quarter * 8 : quarter * 8 + 8, :] = total


def apply_system(fluid, base, jac, cols, dt, table, halo, sums, residual, state):
    cells = fluid.shape[1]

    def step(q, carry):
        where_at, chunk = [], []
        for j in range(4):
            col = cols[:, lanes(q * 4 + j)]
            shifted = col + 64 - q * 512
            far = col - cells
            far_at = (far >> 9) * 16 + (far & 511) - q * 16
            inside = col < cells
            where_at.append(jnp.where(inside, shifted, far_at) & (LANES - 1))
            chunk.append(jnp.where(inside, shifted >> 7, 5))
        picked = [[None] * 5 for _ in range(4)]
        for c in range(5):
            rows = [table[q * 4 + k, c : c + 1, :] for k in range(5)]
            rows.append(halo[c, pl.ds(q, 1), :])
            for j in range(4):
                total = pick(rows[0], where_at[j])
                for k in range(1, 6):
                    total = jnp.where(chunk[j] == k, pick(rows[k], where_at[j]), total)
                picked[j][c] = total
        for j in range(4):
            at = lanes(q * 4 + j)
            for r in range(5):
                total = jac[r, 0, :, at].astype(F32) * picked[j][0]
                for c in range(1, 5):
                    total = total + jac[r, c, :, at].astype(F32) * picked[j][c]
                sums[j, r * 8 : r * 8 + 7, :] = total
            coupled = sums[j, pl.ds(0, 5, stride=8), :]
            for b in range(1, 7):
                coupled = coupled + sums[j, pl.ds(b, 5, stride=8), :]
            left = base[:, at] - coupled
            residual[:, at] = left
            block = q * 4 + j
            state[pl.ds(pl.multiple_of(block * 8, 8), 5), :] = (
                fluid[:, at] + dt[pl.ds(block, 1), :] * left
            )
        return carry

    lax.fori_loop(0, cells // 512, step, 0)


def cell_pressures(state, pressure):
    def step(i, carry):
        first = pl.multiple_of(i * 64, 64)
        p0, p1, p4 = (state[pl.ds(first + r, 8, stride=8), :] for r in (0, 1, 4))
        pressure[pl.ds(pl.multiple_of(i * 8, 8), 8), :] = 0.4 * (p4 - 0.8 * p1 + 0.32 * p0)
        return carry

    lax.fori_loop(0, 16, step, 0, unroll=4)


def face_loads(peers, pressure, cell_at, scale_at, slab):
    groups = peers // 8
    cells = [cell_at[g * 8 : g * 8 + 8, :] for g in range(groups)]
    low = [cell & (LANES - 1) for cell in cells]
    high = [cell >> 7 for cell in cells]

    def step(i, total):
        row = pressure[pl.ds(i, 1), :]
        return tuple(jnp.where(high[g] == i, pick(row, low[g]), total[g]) for g in range(groups))

    found = lax.fori_loop(
        0, 128, step, tuple(jnp.zeros((8, LANES), F32) for _ in range(groups)), unroll=4
    )
    for g in range(groups):
        for c in range(3):
            slab[g * 8 : g * 8 + 8, c, :] = scale_at[c, g * 8 : g * 8 + 8, :] * found[g]


def node_sums(peers, got):
    line = iota((LANES, LANES), 0)
    above = iota((8, LANES), 0) >> 2
    width = 8

    def step(part, total):
        left, right = [], []
        for s in range(width):
            piece = got[part * width + s]
            node = piece[3:4, :].astype(I32)
            twice = jnp.concatenate([piece, piece], axis=0)
            high = jnp.broadcast_to(node >> 7, (8, LANES))
            spread = jnp.concatenate(
                [jnp.where(high == above, twice, 0.0), jnp.where(high == above + 2, twice, 0.0)],
                axis=0,
            )
            left.append(jnp.concatenate(three_parts(spread), axis=0))
            hit = jnp.broadcast_to(node & (LANES - 1), (LANES, LANES)) == line
            right.append(jnp.where(hit, 1.0, 0.0).astype(BF16))
        return total + dot_nt(jnp.concatenate(left, axis=1), jnp.concatenate(right, axis=1))

    total = lax.fori_loop(0, peers // width, step, jnp.zeros((48, LANES), F32))
    return total[0:16, :] + total[16:32, :] + total[32:48, :]


def tile_response(sums, compliance, moved, displacement):
    for t in range(4):
        load = jnp.concatenate([sums[t * 4 + c : t * 4 + c + 1, :] for c in range(3)], axis=1)
        out = dot_nt(jnp.broadcast_to(load, (8, load.shape[1])), compliance[t], HIGH)
        for c in range(3):
            row = out[0:1, c * LANES : (c + 1) * LANES]
            moved[c * 4 + t : c * 4 + t + 1, :] = row
            displacement[c : c + 1, t * LANES : (t + 1) * LANES] = row


def make_replies(peers, got, moved, reply):
    def step(g, carry):
        rows = pl.ds(pl.multiple_of(g * 8, 8), 8)
        node = got[rows, 3, :].astype(I32)
        low, high = node & (LANES - 1), node >> 7
        for c in range(3):
            total = pick(moved[c * 4 : c * 4 + 1, :], low)
            for t in range(1, 4):
                total = jnp.where(high == t, pick(moved[c * 4 + t : c * 4 + t + 1, :], low), total)
            reply[rows, c, :] = total
        return carry

    lax.fori_loop(0, peers // 8, step, 0)


def face_motions(peers, answer, relative, rank, weight, motion):
    slot = [rank[g * 8 : g * 8 + 8, :].astype(I32) for g in range(4)]
    peer = [relative[g * 8 : g * 8 + 8, :] for g in range(4)]

    def step(r, total):
        total = list(total)
        for c in range(3):
            row = answer[r, c : c + 1, :]
            for g in range(4):
                total[c * 4 + g] = jnp.where(peer[g] == r, pick(row, slot[g]), total[c * 4 + g])
        return tuple(total)

    total = lax.fori_loop(
        0, peers, step, tuple(jnp.zeros((8, LANES), F32) for _ in range(12)), unroll=4
    )
    for c in range(3):
        for g in range(4):
            out = total[c * 4 + g] * weight[g * 8 : g * 8 + 8, :]
            for s in range(8):
                at = (g * 8 + s) * LANES
                motion[c : c + 1, at : at + LANES] = out[s : s + 1, :]


INPUTS = ("fluid", "base", "jac", "cols", "dt", "send", "fcell", "area", "weight", "route", "fnode", "comp")


def kernel(peers, *refs):
    count = len(INPUTS)
    hbm = dict(zip(INPUTS, refs[:count]))
    residual_out, displacement, motion = refs[count : count + 3]
    refs = refs[count + 3 :]
    v = dict(zip(INPUTS, refs[:count]))
    (
        index, sends, arrived, table, halo, relative, onehot, prefix, rank, cell_at, scale_at,
        slab, got, sums, residual, state, pressure, moved, reply, answer,
        in_sems, out_sem, halo_send, halo_recv, load_send, load_recv, back_send, back_recv,
    ) = refs[count:]
    me = lax.axis_index("dom")
    copies = {
        name: pltpu.make_async_copy(hbm[name], v[name], in_sems.at[i])
        for i, name in enumerate(INPUTS)
    }
    for name in ("fluid", "send", "route", "fcell", "fnode", "weight", "area", "cols", "jac", "base", "dt", "comp"):
        copies[name].start()
    barrier = pltpu.get_barrier_semaphore()

    def greet(r, carry):
        pl.semaphore_signal(
            barrier, inc=1, device_id={"dom": (me + r) & (peers - 1)}, device_id_type=MESH
        )
        return carry

    lax.fori_loop(1, peers, greet, 0)
    copies["send"].wait()
    copies["fluid"].wait()
    gather_sends(v["fluid"], v["send"], index, sends)
    pl.semaphore_wait(barrier, peers - 1)

    halo_copies = []
    for m in range(6):
        copy = pltpu.make_async_remote_copy(
            src_ref=sends.at[pl.ds(24 * m, 24)],
            dst_ref=arrived.at[5 - m],
            send_sem=halo_send.at[m],
            recv_sem=halo_recv.at[5 - m],
            device_id={"dom": (me + OFFSETS[m] + peers) & (peers - 1)},
            device_id_type=MESH,
        )
        copy.start()
        halo_copies.append(copy)

    shift_table(v["fluid"], table)
    copies["route"].wait()
    rank_faces(me, peers, v["route"], relative, onehot, prefix, rank)
    for name in ("fcell", "fnode", "weight", "area"):
        copies[name].wait()
    compact_faces(
        peers, onehot, rank, v["fcell"], v["fnode"], v["weight"], v["area"], cell_at, slab, scale_at
    )
    for copy in halo_copies:
        copy.wait()
    halo_table(arrived, halo)
    for name in ("cols", "jac", "base", "dt"):
        copies[name].wait()
    apply_system(
        v["fluid"], v["base"], v["jac"], v["cols"], v["dt"], table, halo, sums, residual, state
    )
    residual_copy = pltpu.make_async_copy(residual, residual_out, out_sem)
    residual_copy.start()
    cell_pressures(state, pressure)
    face_loads(peers, pressure, cell_at, scale_at, slab)

    def exchange(source, target, send_sem, recv_sem, sign):
        def one(r):
            return pltpu.make_async_remote_copy(
                src_ref=source.at[r],
                dst_ref=target.at[r],
                send_sem=send_sem,
                recv_sem=recv_sem,
                device_id={"dom": (me + sign * r + peers) & (peers - 1)},
                device_id_type=MESH,
            )

        def start(r, carry):
            one(r).start()
            return carry

        lax.fori_loop(1, peers, start, 0)
        target[0] = source[0]
        return pltpu.make_async_remote_copy(
            src_ref=source.at[pl.ds(1, peers - 1)],
            dst_ref=target.at[pl.ds(1, peers - 1)],
            send_sem=send_sem,
            recv_sem=recv_sem,
            device_id={"dom": (me + 1) & (peers - 1)},
            device_id_type=MESH,
        )

    forth = exchange(slab, got, load_send, load_recv, 1)
    copies["comp"].wait()
    forth.wait()
    tile_response(node_sums(peers, got), v["comp"], moved, displacement)
    make_replies(peers, got, moved, reply)
    back = exchange(reply, answer, back_send, back_recv, -1)
    back.wait()
    face_motions(peers, answer, relative, rank, v["weight"], motion)
    residual_copy.wait()


def per_device(
    fluid_state,
    residual_base,
    jacobian,
    columns,
    pseudo_step,
    send_cells,
    interface_face_cell,
    interface_face_area_vector,
    mortar_weight,
    face_route,
    face_node,
    compliance,
):
    peers = lax.axis_size("dom")
    operands = (
        fluid_state,
        residual_base,
        jnp.transpose(jacobian, (1, 2, 0, 3)),
        columns,
        pseudo_step.reshape(-1, LANES),
        send_cells,
        interface_face_cell.reshape(-1, LANES),
        interface_face_area_vector,
        mortar_weight.reshape(-1, LANES),
        face_route.reshape(-1, LANES),
        face_node.reshape(-1, LANES),
        compliance,
    )
    vmem = pltpu.VMEM
    dma = pltpu.SemaphoreType.DMA
    scratch = [vmem(x.shape, x.dtype) for x in operands] + [
        vmem((8, 512), I32),
        vmem((192, LANES), F32),
        vmem((6, 24, LANES), F32),
        vmem((129, 8, LANES), F32),
        vmem((5, 32, LANES), F32),
        vmem((32, LANES), I32),
        vmem((32 * peers, LANES), BF16),
        vmem((32 * peers, 2 * LANES), F32),
        vmem((32, LANES), F32),
        vmem((peers, LANES), I32),
        vmem((3, peers, LANES), F32),
        vmem((peers, 4, LANES), F32),
        vmem((peers, 4, LANES), F32),
        vmem((4, 40, LANES), F32),
        vmem(fluid_state.shape, F32),
        vmem((1024, LANES), F32),
        vmem((LANES, LANES), F32),
        vmem((16, LANES), F32),
        vmem((peers, 4, LANES), F32),
        vmem((peers, 4, LANES), F32),
        dma((len(INPUTS),)),
        dma,
        dma((6,)),
        dma((6,)),
        dma,
        dma,
        dma,
        dma,
    ]
    return pl.pallas_call(
        functools.partial(kernel, peers),
        out_shape=(
            jax.ShapeDtypeStruct(fluid_state.shape, F32),
            jax.ShapeDtypeStruct((3, compliance.shape[0] * LANES), F32),
            jax.ShapeDtypeStruct(interface_face_area_vector.shape, F32),
        ),
        in_specs=[pl.BlockSpec(memory_space=pl.ANY)] * len(operands),
        out_specs=(
            pl.BlockSpec(memory_space=pl.ANY),
            pl.BlockSpec(memory_space=vmem),
            pl.BlockSpec(memory_space=vmem),
        ),
        scratch_shapes=scratch,
        compiler_params=pltpu.CompilerParams(
            collective_id=0, has_side_effects=True, vmem_limit_bytes=56 * 1024 * 1024
        ),
    )(*operands)


def solution(mesh):
    return jax.shard_map(
        per_device,
        mesh=mesh,
        in_specs=(
            P(None, ("sweep", "dom")),
            P(None, ("sweep", "dom")),
            P(None, None, None, ("sweep", "dom")),
            P(None, ("sweep", "dom")),
            P(("sweep", "dom")),
            P(("sweep", "dom"), None),
            P(("sweep", "dom")),
            P(None, ("sweep", "dom")),
            P(("sweep", "dom")),
            P(("sweep", "dom"), None),
            P(("sweep", "dom")),
            P(("sweep", "dom"), None, None),
        ),
        out_specs=(P(None, ("sweep", "dom")), P(None, ("sweep", "dom")), P(None, ("sweep", "dom"))),
        check_vma=False,
    )
```

time: 472 us -> 69.5 us (0.15)
  local copies, waits for them, and re-layouts: 192 us -> 4.64 us
  matrix products: 157 us -> 0 us
  Pallas kernels: 0 us -> 64 us
  starting transfers between devices: 49.7 us -> 0 us
  other arithmetic: 36.3 us -> 0 us
  waiting for transfers between devices: 21.7 us -> 0 us
  loops' own time: 11 us -> 0 us
    dot_general x24 -> x0, matrix products: 157 us -> none  [the longest x16 130 us: one_block(): return jnp.einsum('cw,biw->cbi', window, onehot, precision=HIGH)]
    gather x114 -> x0, local copies, waits for them, and re-layouts: 132 us -> none
    pallas_call x0 -> x1, Pallas kernels: none -> 64 us  [per_device(): pl.pallas_call(functools.partial(kernel, peers), out_shape=(jax.ShapeDtyp...]
    all_to_all x3 -> x0, starting transfers between devices: 32.9 us -> none  [the longest x1 14.2 us: per_device(): lax.all_to_all(sent_nodes, 'dom', split_axis=1, concat_axis=1, tiled=True)]
    select_n x33 -> x0, other arithmetic: 25.2 us -> none  [the longest x16 23.3 us: one_block(): where_at = jnp.where(inside, local_pos, local_width + halo_pos)]
    all_to_all x3 -> x0, waiting for transfers between devices: 21.7 us -> none  [the longest x1 11 us: per_device(): lax.all_to_all(sent_loads, 'dom', split_axis=1, concat_axis=1, tiled=True)]
    ppermute x6 -> x0, starting transfers between devices: 16.8 us -> none  [from_behind(): return lax.ppermute(block, axis, route)]
    while x97 -> x0, local copies, waits for them, and re-layouts: 15.1 us -> none
  transfers between devices with their start and end apart: 9 -> 0, of which waited for: 2 -> 0; matrix products, arithmetic and copies ran while one was open for 70% -> 0% of each run, Pallas kernels for 0% -> 0%
where the time goes in v1:
time: 69.5 us; the launch traced here: 69.3 us
  Pallas kernels  64 us (92%)
  local copies, waits for them, and re-layouts  4.64 us (7%)
    pallas_call x1, Pallas kernels, per_device(): pl.pallas_call(functools.partial(kernel, peers), out_shape=(jax.ShapeDtyp...  64 us
    unnamed x3, local copies, waits for them, and re-layouts  4.64 us

profile of v1, /device:TPU:1, one launch (start us, length us, event | category | flops | bytes accessed | tf_op | source)
XLA Modules:
  0.0 69.3 jit_solution(5453323775424680600)
XLA Ops:
  0.6 64.0 %shard_map.139 = (f32[5,16384]{1,0:T(8,128)}, f32[3,512]{1,0:T(4,128)}, f32[3,4096]{1,0:T(4,128)}) custom-call(f32[5,16384]{1,0:T(8,128)} %refs_0_.1, f32[5,16384]{1,0:T(8,128)} %refs_1_.1, bf16[5,5,7,16384]{3,2,1,0:T(8,128)(2,1)} %bitcast.6, s32[7,16384]{1,0:T(8,128)} %refs_3_.1, f32[128,128]{1,0:T(8,128)} %bitcast.7, s32[6,512]{1,0:T(8,128)} %refs_5_.1, ...), custom_call_target="tpu_custom_call" | custom-call | tf_op jit(solution)/shard_map/pallas_call | solution.py:479
  64.6 1.9 %copy.18 = f32[5,16384]{1,0:T(8,128)} copy(f32[5,16384]{1,0:T(8,128)} %get-tuple-element.6) | data formatting | bytes 655360
  66.5 1.3 %copy.19 = f32[3,512]{1,0:T(4,128)} copy(f32[3,512]{1,0:T(4,128)} %get-tuple-element.7) | data formatting | bytes 12288
  67.8 1.5 %copy.20 = f32[3,4096]{1,0:T(4,128)} copy(f32[3,4096]{1,0:T(4,128)} %get-tuple-element.8) | data formatting | bytes 98304

commit v2 on v1

--- a/solution.py
+++ b/solution.py
@@ -44,27 +44,31 @@
     )
 
 
-def gather_sends(fluid, send, index, out):
-    index[0:6, :] = send[...]
-    index[6:8, :] = jnp.zeros((2, index.shape[1]), I32)
-    cells = [index[:, k * LANES : (k + 1) * LANES] for k in range(4)]
-    low = [cell & (LANES - 1) for cell in cells]
-    high = [cell >> 7 for cell in cells]
-
-    def step(block, total):
-        total = list(total)
-        hit = [h == block for h in high]
+def gather_sends(fluid, send, index, found, out):
+    for k in range(4):
+        index[pl.ds(k, 6, stride=4), :] = send[:, k * LANES : (k + 1) * LANES]
+
+    def part(g, carry):
+        rows = pl.ds(pl.multiple_of(g * 8, 8), 8)
+        cell = index[rows, :]
+        low, high = cell & (LANES - 1), cell >> 7
+
+        def step(block, total):
+            hit = high == block
+            return tuple(
+                jnp.where(hit, pick(fluid[pl.ds(c, 1), lanes(block)], low), total[c])
+                for c in range(5)
+            )
+
+        total = lax.fori_loop(0, 128, step, (jnp.zeros((8, LANES), F32),) * 5, unroll=128)
         for c in range(5):
-            row = fluid[pl.ds(c, 1), lanes(block)]
-            for k in range(4):
-                total[c * 4 + k] = jnp.where(hit[k], pick(row, low[k]), total[c * 4 + k])
-        return tuple(total)
-
-    total = lax.fori_loop(
-        0, 128, step, tuple(jnp.zeros((8, LANES), F32) for _ in range(20)), unroll=4
-    )
-    for slot in range(20):
-        out[pl.ds(slot, 8, stride=24), :] = total[slot]
+            found[c, rows, :] = total[c]
+        return carry
+
+    lax.fori_loop(0, 3, part, 0)
+    for m in range(6):
+        for c in range(5):
+            out[m * 24 + c * 4 : m * 24 + c * 4 + 4, :] = found[c, m * 4 : m * 4 + 4, :]
 
 
 def shift_table(fluid, table):
@@ -75,7 +79,7 @@
         table[block, 0:5, :] = jnp.where(left, before, here)
         return here
 
-    last = lax.fori_loop(0, 128, step, jnp.zeros((5, LANES), F32), unroll=4)
+    last = lax.fori_loop(0, 128, step, jnp.zeros((5, LANES), F32), unroll=32)
     table[128, 0:5, :] = last
 
 
@@ -105,7 +109,7 @@
     lax.fori_loop(0, 32, step, jnp.zeros((peers, LANES), F32), unroll=2)
 
 
-def compact_faces(peers, onehot, rank, fcell, fnode, weight, area, cell_at, slab, scale_at):
+def compact_faces(peers, onehot, rank, fcell, fnode, weight, area, face_at, cell_at, slab, scale_at):
     line = iota((LANES, LANES), 0).astype(F32)
     lane = iota((peers, LANES), 1).astype(F32)
 
@@ -126,31 +130,36 @@
     found = lax.fori_loop(0, 16, step, jnp.zeros((2 * peers, LANES), F32))
     high = found[0:peers, :].astype(I32) - 1
     low = found[peers : 2 * peers, :].astype(I32)
-    groups = peers // 8
-    for g in range(groups):
-        h = high[g * 8 : g * 8 + 8, :]
-        l = low[g * 8 : g * 8 + 8, :]
-
-        def look(i, total, h=h, l=l):
+    face_at[...] = (high << 7) + low
+
+    def part(g, carry):
+        rows = pl.ds(pl.multiple_of(g * 8, 8), 8)
+        face = face_at[rows, :]
+        h, l = face >> 7, face & (LANES - 1)
+
+        def look(i, total):
             hit = h == i
-            rows = (
+            pieces = (
                 fcell[pl.ds(i, 1), :],
                 fnode[pl.ds(i, 1), :],
                 weight[pl.ds(i, 1), :] * area[0:1, lanes(i)],
                 weight[pl.ds(i, 1), :] * area[1:2, lanes(i)],
                 weight[pl.ds(i, 1), :] * area[2:3, lanes(i)],
             )
-            return tuple(jnp.where(hit, pick(row, l), old) for row, old in zip(rows, total))
+            return tuple(jnp.where(hit, pick(row, l), old) for row, old in zip(pieces, total))
 
         none_i = jnp.zeros((8, LANES), I32)
         none_f = jnp.zeros((8, LANES), F32)
         cell, node, *scales = lax.fori_loop(
-            0, 32, look, (none_i, none_i, none_f, none_f, none_f), unroll=8
+            0, 32, look, (none_i, none_i, none_f, none_f, none_f), unroll=32
         )
-        cell_at[g * 8 : g * 8 + 8, :] = cell
-        slab[g * 8 : g * 8 + 8, 3, :] = node.astype(F32)
+        cell_at[rows, :] = cell
+        slab[rows, 3, :] = node.astype(F32)
         for c in range(3):
-            scale_at[c, g * 8 : g * 8 + 8, :] = scales[c]
+            scale_at[c, rows, :] = scales[c]
+        return carry
+
+    lax.fori_loop(0, peers // 8, part, 0)
 
 
 def halo_table(arrived, table):
@@ -178,21 +187,20 @@
             inside = col < cells
             where_at.append(jnp.where(inside, shifted, far_at) & (LANES - 1))
             chunk.append(jnp.where(inside, shifted >> 7, 5))
-        picked = [[None] * 5 for _ in range(4)]
-        for c in range(5):
-            rows = [table[q * 4 + k, c : c + 1, :] for k in range(5)]
-            rows.append(halo[c, pl.ds(q, 1), :])
-            for j in range(4):
-                total = pick(rows[0], where_at[j])
-                for k in range(1, 6):
-                    total = jnp.where(chunk[j] == k, pick(rows[k], where_at[j]), total)
-                picked[j][c] = total
         for j in range(4):
+            picked = []
+            for c in range(5):
+                total = pick(table[q * 4, c : c + 1, :], where_at[j])
+                for k in range(1, 5):
+                    got = pick(table[q * 4 + k, c : c + 1, :], where_at[j])
+                    total = jnp.where(chunk[j] == k, got, total)
+                got = pick(halo[c, pl.ds(q, 1), :], where_at[j])
+                picked.append(jnp.where(chunk[j] == 5, got, total))
             at = lanes(q * 4 + j)
             for r in range(5):
-                total = jac[r, 0, :, at].astype(F32) * picked[j][0]
+                total = jac[r, 0, :, at].astype(F32) * picked[0]
                 for c in range(1, 5):
-                    total = total + jac[r, c, :, at].astype(F32) * picked[j][c]
+                    total = total + jac[r, c, :, at].astype(F32) * picked[c]
                 sums[j, r * 8 : r * 8 + 7, :] = total
             coupled = sums[j, pl.ds(0, 5, stride=8), :]
             for b in range(1, 7):
@@ -219,21 +227,20 @@
 
 
 def face_loads(peers, pressure, cell_at, scale_at, slab):
-    groups = peers // 8
-    cells = [cell_at[g * 8 : g * 8 + 8, :] for g in range(groups)]
-    low = [cell & (LANES - 1) for cell in cells]
-    high = [cell >> 7 for cell in cells]
-
-    def step(i, total):
-        row = pressure[pl.ds(i, 1), :]
-        return tuple(jnp.where(high[g] == i, pick(row, low[g]), total[g]) for g in range(groups))
-
-    found = lax.fori_loop(
-        0, 128, step, tuple(jnp.zeros((8, LANES), F32) for _ in range(groups)), unroll=4
-    )
-    for g in range(groups):
+    def part(g, carry):
+        rows = pl.ds(pl.multiple_of(g * 8, 8), 8)
+        cell = cell_at[rows, :]
+        low, high = cell & (LANES - 1), cell >> 7
+
+        def step(i, total):
+            return jnp.where(high == i, pick(pressure[pl.ds(i, 1), :], low), total)
+
+        found = lax.fori_loop(0, 128, step, jnp.zeros((8, LANES), F32), unroll=128)
         for c in range(3):
-            slab[g * 8 : g * 8 + 8, c, :] = scale_at[c, g * 8 : g * 8 + 8, :] * found[g]
+            slab[rows, c, :] = scale_at[c, rows, :] * found
+        return carry
+
+    lax.fori_loop(0, peers // 8, part, 0)
 
 
 def node_sums(peers, got):
@@ -287,23 +294,19 @@
 
 
 def face_motions(peers, answer, relative, rank, weight, motion):
-    slot = [rank[g * 8 : g * 8 + 8, :].astype(I32) for g in range(4)]
-    peer = [relative[g * 8 : g * 8 + 8, :] for g in range(4)]
-
-    def step(r, total):
-        total = list(total)
+    for g in range(4):
+        rows = slice(g * 8, g * 8 + 8)
+        slot, peer = rank[rows, :].astype(I32), relative[rows, :]
+
+        def step(r, total, slot=slot, peer=peer):
+            hit = peer == r
+            return tuple(
+                jnp.where(hit, pick(answer[r, c : c + 1, :], slot), total[c]) for c in range(3)
+            )
+
+        total = lax.fori_loop(0, peers, step, (jnp.zeros((8, LANES), F32),) * 3, unroll=peers)
         for c in range(3):
-            row = answer[r, c : c + 1, :]
-            for g in range(4):
-                total[c * 4 + g] = jnp.where(peer[g] == r, pick(row, slot[g]), total[c * 4 + g])
-        return tuple(total)
-
-    total = lax.fori_loop(
-        0, peers, step, tuple(jnp.zeros((8, LANES), F32) for _ in range(12)), unroll=4
-    )
-    for c in range(3):
-        for g in range(4):
-            out = total[c * 4 + g] * weight[g * 8 : g * 8 + 8, :]
+            out = total[c] * weight[rows, :]
             for s in range(8):
                 at = (g * 8 + s) * LANES
                 motion[c : c + 1, at : at + LANES] = out[s : s + 1, :]
@@ -319,7 +322,7 @@
     refs = refs[count + 3 :]
     v = dict(zip(INPUTS, refs[:count]))
     (
-        index, sends, arrived, table, halo, relative, onehot, prefix, rank, cell_at, scale_at,
+        index, found, sends, arrived, table, halo, relative, onehot, prefix, rank, face_at, cell_at, scale_at,
         slab, got, sums, residual, state, pressure, moved, reply, answer,
         in_sems, out_sem, halo_send, halo_recv, load_send, load_recv, back_send, back_recv,
     ) = refs[count:]
@@ -341,7 +344,7 @@
     lax.fori_loop(1, peers, greet, 0)
     copies["send"].wait()
     copies["fluid"].wait()
-    gather_sends(v["fluid"], v["send"], index, sends)
+    gather_sends(v["fluid"], v["send"], index, found, sends)
     pl.semaphore_wait(barrier, peers - 1)
 
     halo_copies = []
@@ -363,7 +366,8 @@
     for name in ("fcell", "fnode", "weight", "area"):
         copies[name].wait()
     compact_faces(
-        peers, onehot, rank, v["fcell"], v["fnode"], v["weight"], v["area"], cell_at, slab, scale_at
+        peers, onehot, rank, v["fcell"], v["fnode"], v["weight"], v["area"],
+        face_at, cell_at, slab, scale_at,
     )
     for copy in halo_copies:
         copy.wait()
@@ -447,7 +451,8 @@
     vmem = pltpu.VMEM
     dma = pltpu.SemaphoreType.DMA
     scratch = [vmem(x.shape, x.dtype) for x in operands] + [
-        vmem((8, 512), I32),
+        vmem((24, LANES), I32),
+        vmem((5, 24, LANES), F32),
         vmem((192, LANES), F32),
         vmem((6, 24, LANES), F32),
         vmem((129, 8, LANES), F32),
@@ -456,6 +461,7 @@
         vmem((32 * peers, LANES), BF16),
         vmem((32 * peers, 2 * LANES), F32),
         vmem((32, LANES), F32),
+        vmem((peers, LANES), I32),
         vmem((peers, LANES), I32),
         vmem((3, peers, LANES), F32),
         vmem((peers, 4, LANES), F32),

time: 69.5 us -> 53.8 us (0.77)
  Pallas kernels: 64 us -> 48.3 us
    pallas_call x1, Pallas kernels: 64 us -> 48.3 us  [per_device(): pl.pallas_call(functools.partial(kernel, peers), out_shape=(jax.ShapeDtyp...]
where the time goes in v2:
time: 53.8 us; the launch traced here: 53.6 us
  Pallas kernels  48.3 us (90%)
  local copies, waits for them, and re-layouts  4.64 us (9%)
  between operations  0.64 us (1%)
    pallas_call x1, Pallas kernels, per_device(): pl.pallas_call(functools.partial(kernel, peers), out_shape=(jax.ShapeDtyp...  48.3 us
    unnamed x3, local copies, waits for them, and re-layouts  4.64 us

profile of v2, /device:TPU:1, one launch (start us, length us, event | category | flops | bytes accessed | tf_op | source)
XLA Modules:
  0.0 53.6 jit_solution(1730829422228498321)
XLA Ops:
  0.6 48.3 %shard_map.139 = (f32[5,16384]{1,0:T(8,128)}, f32[3,512]{1,0:T(4,128)}, f32[3,4096]{1,0:T(4,128)}) custom-call(f32[5,16384]{1,0:T(8,128)} %refs_0_.1, f32[5,16384]{1,0:T(8,128)} %refs_1_.1, bf16[5,5,7,16384]{3,2,1,0:T(8,128)(2,1)} %bitcast.6, s32[7,16384]{1,0:T(8,128)} %refs_3_.1, f32[128,128]{1,0:T(8,128)} %bitcast.7, s32[6,512]{1,0:T(8,128)} %refs_5_.1, ...), custom_call_target="tpu_custom_call" | custom-call | tf_op jit(solution)/shard_map/pallas_call | solution.py:485
  49.0 1.9 %copy.18 = f32[5,16384]{1,0:T(8,128)} copy(f32[5,16384]{1,0:T(8,128)} %get-tuple-element.6) | data formatting | bytes 655360
  50.8 1.3 %copy.19 = f32[3,512]{1,0:T(4,128)} copy(f32[3,512]{1,0:T(4,128)} %get-tuple-element.7) | data formatting | bytes 12288
  52.1 1.5 %copy.20 = f32[3,4096]{1,0:T(4,128)} copy(f32[3,4096]{1,0:T(4,128)} %get-tuple-element.8) | data formatting | bytes 98304

commit v3 on v2

--- a/solution.py
+++ b/solution.py
@@ -44,6 +44,22 @@
     )
 
 
+def offset_of(group, place):
+    side = place // 2
+    dz = 4 + (1 - 2 * (group % 2)) * ((group + 1) // 2)
+    dy = 2 + (1 - 2 * (side % 2)) * ((side + 1) // 2)
+    return dz, dy, 1 - place % 2
+
+
+def slot_of(me, route):
+    dz = ((route >> 3) - (me >> 3)) & 7
+    dy = ((route >> 1) - (me >> 1)) & 3
+    dc = (route - me) & 1
+    group = jnp.where(dz < 4, 7 - 2 * dz, 2 * dz - 8)
+    side = jnp.where(dy < 2, 3 - 2 * dy, 2 * dy - 4)
+    return group * 8 + side * 2 + (1 - dc)
+
+
 def gather_sends(fluid, send, index, found, out):
     for k in range(4):
         index[pl.ds(k, 6, stride=4), :] = send[:, k * LANES : (k + 1) * LANES]
@@ -84,7 +100,7 @@
 
 
 def rank_faces(me, peers, route, relative, onehot, prefix, rank):
-    relative[...] = (route[...] - me) & (peers - 1)
+    relative[...] = slot_of(me, route[...])
     line = iota((peers, LANES), 0)
     for i in range(32):
         hit = jnp.broadcast_to(relative[i : i + 1, :], (peers, LANES)) == line
@@ -109,7 +125,7 @@
     lax.fori_loop(0, 32, step, jnp.zeros((peers, LANES), F32), unroll=2)
 
 
-def compact_faces(peers, onehot, rank, fcell, fnode, weight, area, face_at, cell_at, slab, scale_at):
+def compact_faces(peers, onehot, rank, fnode, weight, area, face_at, slab, scale):
     line = iota((LANES, LANES), 0).astype(F32)
     lane = iota((peers, LANES), 1).astype(F32)
 
@@ -127,7 +143,7 @@
             right.append(jnp.where(place, 1.0, 0.0).astype(BF16))
         return total + dot_nt(jnp.concatenate(left, axis=1), jnp.concatenate(right, axis=1))
 
-    found = lax.fori_loop(0, 16, step, jnp.zeros((2 * peers, LANES), F32))
+    found = lax.fori_loop(0, 16, step, jnp.zeros((2 * peers, LANES), F32), unroll=COMPACT_UNROLL)
     high = found[0:peers, :].astype(I32) - 1
     low = found[peers : 2 * peers, :].astype(I32)
     face_at[...] = (high << 7) + low
@@ -138,28 +154,19 @@
         h, l = face >> 7, face & (LANES - 1)
 
         def look(i, total):
-            hit = h == i
-            pieces = (
-                fcell[pl.ds(i, 1), :],
-                fnode[pl.ds(i, 1), :],
-                weight[pl.ds(i, 1), :] * area[0:1, lanes(i)],
-                weight[pl.ds(i, 1), :] * area[1:2, lanes(i)],
-                weight[pl.ds(i, 1), :] * area[2:3, lanes(i)],
-            )
-            return tuple(jnp.where(hit, pick(row, l), old) for row, old in zip(pieces, total))
-
-        none_i = jnp.zeros((8, LANES), I32)
-        none_f = jnp.zeros((8, LANES), F32)
-        cell, node, *scales = lax.fori_loop(
-            0, 32, look, (none_i, none_i, none_f, none_f, none_f), unroll=32
-        )
-        cell_at[rows, :] = cell
+            return jnp.where(h == i, pick(fnode[pl.ds(i, 1), :], l), total)
+
+        node = lax.fori_loop(0, 32, look, jnp.zeros((8, LANES), I32), unroll=32)
         slab[rows, 3, :] = node.astype(F32)
-        for c in range(3):
-            scale_at[c, rows, :] = scales[c]
-        return carry
-
-    lax.fori_loop(0, peers // 8, part, 0)
+        return carry
+
+    lax.fori_loop(0, peers // 8, part, 0, unroll=2)
+
+    def weigh(i, carry):
+        scale[pl.ds(i, 3, stride=32), :] = weight[pl.ds(i, 1), :] * area[:, lanes(i)]
+        return carry
+
+    lax.fori_loop(0, 32, weigh, 0, unroll=8)
 
 
 def halo_table(arrived, table):
@@ -174,8 +181,9 @@
             table[c, quarter * 8 : quarter * 8 + 8, :] = total
 
 
-def apply_system(fluid, base, jac, cols, dt, table, halo, sums, residual, state):
+def apply_system(fluid, base, jac, cols, dt, table, halo, sums, picks, residual, state):
     cells = fluid.shape[1]
+    sums[...] = jnp.zeros(sums.shape, F32)
 
     def step(q, carry):
         where_at, chunk = [], []
@@ -197,7 +205,9 @@
                 got = pick(halo[c, pl.ds(q, 1), :], where_at[j])
                 picked.append(jnp.where(chunk[j] == 5, got, total))
             at = lanes(q * 4 + j)
-            for r in range(5):
+            for c in range(5):
+                picks[c, q * 4 + j, 0:7, :] = picked[c]
+            for r in (0, 1, 4):
                 total = jac[r, 0, :, at].astype(F32) * picked[0]
                 for c in range(1, 5):
                     total = total + jac[r, c, :, at].astype(F32) * picked[c]
@@ -213,7 +223,26 @@
             )
         return carry
 
-    lax.fori_loop(0, cells // 512, step, 0)
+    lax.fori_loop(0, cells // 512, step, 0, unroll=APPLY_UNROLL)
+
+
+def apply_rest(base, jac, picks, sums, residual):
+    def step(quad, carry):
+        for j in range(4):
+            block = quad * 4 + j
+            at = lanes(block)
+            for r in (2, 3):
+                total = jac[r, 0, :, at].astype(F32) * picks[0, block, 0:7, :]
+                for c in range(1, 5):
+                    total = total + jac[r, c, :, at].astype(F32) * picks[c, block, 0:7, :]
+                sums[j, r * 8 : r * 8 + 7, :] = total
+            coupled = sums[j, pl.ds(0, 5, stride=8), :]
+            for b in range(1, 7):
+                coupled = coupled + sums[j, pl.ds(b, 5, stride=8), :]
+            residual[2:4, at] = (base[:, at] - coupled)[2:4, :]
+        return carry
+
+    lax.fori_loop(0, 32, step, 0)
 
 
 def cell_pressures(state, pressure):
@@ -226,10 +255,10 @@
     lax.fori_loop(0, 16, step, 0, unroll=4)
 
 
-def face_loads(peers, pressure, cell_at, scale_at, slab):
+def face_loads(pressure, fcell, scale, loads):
     def part(g, carry):
-        rows = pl.ds(pl.multiple_of(g * 8, 8), 8)
-        cell = cell_at[rows, :]
+        first = pl.multiple_of(g * 8, 8)
+        cell = fcell[pl.ds(first, 8), :]
         low, high = cell & (LANES - 1), cell >> 7
 
         def step(i, total):
@@ -237,81 +266,111 @@
 
         found = lax.fori_loop(0, 128, step, jnp.zeros((8, LANES), F32), unroll=128)
         for c in range(3):
-            slab[rows, c, :] = scale_at[c, rows, :] * found
-        return carry
-
-    lax.fori_loop(0, peers // 8, part, 0)
-
-
-def node_sums(peers, got):
+            rows = pl.ds(first + c * 32, 8)
+            loads[rows, :] = scale[rows, :] * found
+        return carry
+
+    lax.fori_loop(0, 4, part, 0)
+
+
+def fill_slabs(g, loads, face_at, slab):
+    rows = pl.ds(pl.multiple_of(g * 8, 8), 8)
+    face = face_at[rows, :]
+    h, l = face >> 7, face & (LANES - 1)
+
+    def look(i, total):
+        hit = h == i
+        return tuple(
+            jnp.where(hit, pick(loads[pl.ds(c * 32 + i, 1), :], l), total[c]) for c in range(3)
+        )
+
+    total = lax.fori_loop(0, 32, look, (jnp.zeros((8, LANES), F32),) * 3, unroll=32)
+    for c in range(3):
+        slab[rows, c, :] = total[c]
+
+
+def node_sums(g, got):
     line = iota((LANES, LANES), 0)
     above = iota((8, LANES), 0) >> 2
-    width = 8
-
-    def step(part, total):
-        left, right = [], []
-        for s in range(width):
-            piece = got[part * width + s]
-            node = piece[3:4, :].astype(I32)
-            twice = jnp.concatenate([piece, piece], axis=0)
-            high = jnp.broadcast_to(node >> 7, (8, LANES))
-            spread = jnp.concatenate(
-                [jnp.where(high == above, twice, 0.0), jnp.where(high == above + 2, twice, 0.0)],
-                axis=0,
-            )
-            left.append(jnp.concatenate(three_parts(spread), axis=0))
-            hit = jnp.broadcast_to(node & (LANES - 1), (LANES, LANES)) == line
-            right.append(jnp.where(hit, 1.0, 0.0).astype(BF16))
-        return total + dot_nt(jnp.concatenate(left, axis=1), jnp.concatenate(right, axis=1))
-
-    total = lax.fori_loop(0, peers // width, step, jnp.zeros((48, LANES), F32))
-    return total[0:16, :] + total[16:32, :] + total[32:48, :]
-
-
-def tile_response(sums, compliance, moved, displacement):
+    left, right = [], []
+    for s in range(8):
+        piece = got[g * 8 + s]
+        node = piece[3:4, :].astype(I32)
+        twice = jnp.concatenate([piece, piece], axis=0)
+        high = jnp.broadcast_to(node >> 7, (8, LANES))
+        spread = jnp.concatenate(
+            [jnp.where(high == above, twice, 0.0), jnp.where(high == above + 2, twice, 0.0)],
+            axis=0,
+        )
+        left.append(jnp.concatenate(three_parts(spread), axis=0))
+        hit = jnp.broadcast_to(node & (LANES - 1), (LANES, LANES)) == line
+        right.append(jnp.where(hit, 1.0, 0.0).astype(BF16))
+    return dot_nt(jnp.concatenate(left, axis=1), jnp.concatenate(right, axis=1))
+
+
+def split_compliance(compliance, high, middle):
+    def step(i, carry):
+        t, rows = i // 4, pl.ds(pl.multiple_of((i % 4) * 96, 96), 96)
+        value = compliance[t, rows, :]
+        top = value.astype(BF16)
+        high[t, rows, :] = top
+        middle[t, rows, :] = (value - top.astype(F32)).astype(BF16)
+        return carry
+
+    lax.fori_loop(0, 16, step, 0)
+
+
+def tile_response(total, high, middle, moved, displacement):
+    sums = total[0:16, :] + total[16:32, :] + total[32:48, :]
     for t in range(4):
         load = jnp.concatenate([sums[t * 4 + c : t * 4 + c + 1, :] for c in range(3)], axis=1)
-        out = dot_nt(jnp.broadcast_to(load, (8, load.shape[1])), compliance[t], HIGH)
+        parts = jnp.concatenate(
+            [jnp.broadcast_to(part, (16, part.shape[1])) for part in three_parts(load)], axis=0
+        )
+        first = dot_nt(parts, high[t])
+        second = dot_nt(parts[0:32], middle[t])
+        out = first[0:1] + ((first[16:17] + second[0:1]) + (first[32:33] + second[16:17]))
         for c in range(3):
-            row = out[0:1, c * LANES : (c + 1) * LANES]
+            row = out[:, c * LANES : (c + 1) * LANES]
             moved[c * 4 + t : c * 4 + t + 1, :] = row
             displacement[c : c + 1, t * LANES : (t + 1) * LANES] = row
 
 
-def make_replies(peers, got, moved, reply):
-    def step(g, carry):
-        rows = pl.ds(pl.multiple_of(g * 8, 8), 8)
-        node = got[rows, 3, :].astype(I32)
-        low, high = node & (LANES - 1), node >> 7
+def make_replies(g, got, moved, reply):
+    rows = pl.ds(pl.multiple_of(g * 8, 8), 8)
+    node = got[rows, 3, :].astype(I32)
+    low, high = node & (LANES - 1), node >> 7
+    for c in range(3):
+        total = pick(moved[c * 4 : c * 4 + 1, :], low)
+        for t in range(1, 4):
+            total = jnp.where(high == t, pick(moved[c * 4 + t : c * 4 + t + 1, :], low), total)
+        reply[rows, c, :] = total
+
+
+def face_motions(g, total, answer, relative, rank):
+    total = list(total)
+    for f in range(4):
+        rows = slice(f * 8, f * 8 + 8)
+        slot, peer = rank[rows, :].astype(I32), relative[rows, :]
+        for s in range(8):
+            hit = peer == g * 8 + s
+            for c in range(3):
+                row = answer[g * 8 + s, c : c + 1, :]
+                total[c * 4 + f] = jnp.where(hit, pick(row, slot), total[c * 4 + f])
+    return tuple(total)
+
+
+def store_motions(total, weight, motion):
+    for f in range(4):
         for c in range(3):
-            total = pick(moved[c * 4 : c * 4 + 1, :], low)
-            for t in range(1, 4):
-                total = jnp.where(high == t, pick(moved[c * 4 + t : c * 4 + t + 1, :], low), total)
-            reply[rows, c, :] = total
-        return carry
-
-    lax.fori_loop(0, peers // 8, step, 0)
-
-
-def face_motions(peers, answer, relative, rank, weight, motion):
-    for g in range(4):
-        rows = slice(g * 8, g * 8 + 8)
-        slot, peer = rank[rows, :].astype(I32), relative[rows, :]
-
-        def step(r, total, slot=slot, peer=peer):
-            hit = peer == r
-            return tuple(
-                jnp.where(hit, pick(answer[r, c : c + 1, :], slot), total[c]) for c in range(3)
-            )
-
-        total = lax.fori_loop(0, peers, step, (jnp.zeros((8, LANES), F32),) * 3, unroll=peers)
-        for c in range(3):
-            out = total[c] * weight[rows, :]
+            out = total[c * 4 + f] * weight[f * 8 : f * 8 + 8, :]
             for s in range(8):
-                at = (g * 8 + s) * LANES
+                at = (f * 8 + s) * LANES
                 motion[c : c + 1, at : at + LANES] = out[s : s + 1, :]
 
 
+APPLY_UNROLL = 4
+COMPACT_UNROLL = 16
 INPUTS = ("fluid", "base", "jac", "cols", "dt", "send", "fcell", "area", "weight", "route", "fnode", "comp")
 
 
@@ -322,8 +381,9 @@
     refs = refs[count + 3 :]
     v = dict(zip(INPUTS, refs[:count]))
     (
-        index, found, sends, arrived, table, halo, relative, onehot, prefix, rank, face_at, cell_at, scale_at,
-        slab, got, sums, residual, state, pressure, moved, reply, answer,
+        index, found, sends, arrived, table, halo, relative, onehot, prefix, rank, face_at, scale,
+        loads, slab, got, sums, picks, residual, state, pressure, comp_high, comp_middle, moved,
+        reply, answer,
         in_sems, out_sem, halo_send, halo_recv, load_send, load_recv, back_send, back_recv,
     ) = refs[count:]
     me = lax.axis_index("dom")
@@ -363,59 +423,96 @@
     shift_table(v["fluid"], table)
     copies["route"].wait()
     rank_faces(me, peers, v["route"], relative, onehot, prefix, rank)
-    for name in ("fcell", "fnode", "weight", "area"):
+    for name in ("fnode", "weight", "area"):
         copies[name].wait()
     compact_faces(
-        peers, onehot, rank, v["fcell"], v["fnode"], v["weight"], v["area"],
-        face_at, cell_at, slab, scale_at,
+        peers, onehot, rank, v["fnode"], v["weight"], v["area"], face_at, slab, scale
     )
     for copy in halo_copies:
         copy.wait()
     halo_table(arrived, halo)
-    for name in ("cols", "jac", "base", "dt"):
+    for name in ("cols", "jac", "base", "dt", "fcell"):
         copies[name].wait()
     apply_system(
-        v["fluid"], v["base"], v["jac"], v["cols"], v["dt"], table, halo, sums, residual, state
+        v["fluid"], v["base"], v["jac"], v["cols"], v["dt"], table, halo, sums, picks, residual, state
     )
+    cell_pressures(state, pressure)
+    face_loads(pressure, v["fcell"], scale, loads)
+
+    def copy_of(source, target, send_sem, recv_sem, slots, to, group):
+        return pltpu.make_async_remote_copy(
+            src_ref=source.at[slots],
+            dst_ref=target.at[slots],
+            send_sem=send_sem,
+            recv_sem=recv_sem.at[group],
+            device_id={"dom": to},
+            device_id_type=MESH,
+        )
+
+    def send_group(source, target, send_sem, recv_sem, sign, group, amount):
+        for place in range(amount):
+            dz, dy, dc = offset_of(group, place)
+            to = (
+                (((me >> 3) + sign * dz + 8) & 7) * 8
+                + (((me >> 1) + sign * dy + 4) & 3) * 2
+                + ((me + dc) & 1)
+            )
+            copy_of(source, target, send_sem, recv_sem, group * 8 + place, to, group).start()
+
+    def received(source, target, send_sem, recv_sem, group, amount):
+        slots = pl.ds(group * 8, amount)
+        copy_of(source, target, send_sem, recv_sem, slots, me ^ 1, group).wait_recv()
+
+    forth = (slab, got, load_send, load_recv)
+    back = (reply, answer, back_send, back_recv)
+
+    def send_loads(g, carry):
+        fill_slabs(g, loads, face_at, slab)
+        send_group(*forth, 1, g, 8)
+        return carry
+
+    lax.fori_loop(0, 7, send_loads, 0)
+    fill_slabs(7, loads, face_at, slab)
+    send_group(*forth, 1, 7, 7)
+    got[63] = slab[63]
+
+    apply_rest(v["base"], v["jac"], picks, sums, residual)
     residual_copy = pltpu.make_async_copy(residual, residual_out, out_sem)
     residual_copy.start()
-    cell_pressures(state, pressure)
-    face_loads(peers, pressure, cell_at, scale_at, slab)
-
-    def exchange(source, target, send_sem, recv_sem, sign):
-        def one(r):
-            return pltpu.make_async_remote_copy(
-                src_ref=source.at[r],
-                dst_ref=target.at[r],
-                send_sem=send_sem,
-                recv_sem=recv_sem,
-                device_id={"dom": (me + sign * r + peers) & (peers - 1)},
-                device_id_type=MESH,
-            )
-
-        def start(r, carry):
-            one(r).start()
-            return carry
-
-        lax.fori_loop(1, peers, start, 0)
-        target[0] = source[0]
-        return pltpu.make_async_remote_copy(
-            src_ref=source.at[pl.ds(1, peers - 1)],
-            dst_ref=target.at[pl.ds(1, peers - 1)],
-            send_sem=send_sem,
-            recv_sem=recv_sem,
-            device_id={"dom": (me + 1) & (peers - 1)},
-            device_id_type=MESH,
-        )
-
-    forth = exchange(slab, got, load_send, load_recv, 1)
     copies["comp"].wait()
-    forth.wait()
-    tile_response(node_sums(peers, got), v["comp"], moved, displacement)
-    make_replies(peers, got, moved, reply)
-    back = exchange(reply, answer, back_send, back_recv, -1)
-    back.wait()
-    face_motions(peers, answer, relative, rank, v["weight"], motion)
+    split_compliance(v["comp"], comp_high, comp_middle)
+
+    received(*forth, 7, 7)
+    total = node_sums(7, got)
+
+    def take_loads(i, total):
+        received(*forth, 6 - i, 8)
+        return total + node_sums(6 - i, got)
+
+    total = lax.fori_loop(0, 7, take_loads, total)
+    tile_response(total, comp_high, comp_middle, moved, displacement)
+
+    def send_replies(g, carry):
+        make_replies(g, got, moved, reply)
+        send_group(*back, -1, g, 8)
+        return carry
+
+    lax.fori_loop(0, 7, send_replies, 0)
+    make_replies(7, got, moved, reply)
+    send_group(*back, -1, 7, 7)
+    answer[63] = reply[63]
+
+    received(*back, 7, 7)
+    motions = face_motions(7, (jnp.zeros((8, LANES), F32),) * 12, answer, relative, rank)
+
+    def take_replies(i, total):
+        received(*back, 6 - i, 8)
+        return face_motions(6 - i, total, answer, relative, rank)
+
+    motions = lax.fori_loop(0, 7, take_replies, motions)
+    store_motions(motions, v["weight"], motion)
+    for source, target, send_sem, recv_sem in (forth, back):
+        copy_of(source, target, send_sem, recv_sem, pl.ds(0, 63), me ^ 1, 0).wait_send()
     residual_copy.wait()
 
 
@@ -462,14 +559,17 @@
         vmem((32 * peers, 2 * LANES), F32),
         vmem((32, LANES), F32),
         vmem((peers, LANES), I32),
-        vmem((peers, LANES), I32),
-        vmem((3, peers, LANES), F32),
+        vmem((96, LANES), F32),
+        vmem((96, LANES), F32),
         vmem((peers, 4, LANES), F32),
         vmem((peers, 4, LANES), F32),
         vmem((4, 40, LANES), F32),
+        vmem((5, 128, 8, LANES), F32),
         vmem(fluid_state.shape, F32),
         vmem((1024, LANES), F32),
         vmem((LANES, LANES), F32),
+        vmem(compliance.shape, BF16),
+        vmem(compliance.shape, BF16),
         vmem((16, LANES), F32),
         vmem((peers, 4, LANES), F32),
         vmem((peers, 4, LANES), F32),
@@ -478,9 +578,9 @@
         dma((6,)),
         dma((6,)),
         dma,
+        dma((8,)),
         dma,
-        dma,
-        dma,
+        dma((8,)),
     ]
     return pl.pallas_call(
         functools.partial(kernel, peers),

time: 53.8 us -> 45.4 us (0.84)
  Pallas kernels: 48.3 us -> 39.9 us
    pallas_call x1, Pallas kernels: 48.3 us -> 39.9 us  [per_device(): pl.pallas_call(functools.partial(kernel, peers), out_shape=(jax.ShapeDtyp...]
where the time goes in v3:
time: 45.4 us; the launch traced here: 45.2 us
  Pallas kernels  39.9 us (88%)
  local copies, waits for them, and re-layouts  4.64 us (10%)
  between operations  0.64 us (1%)
    pallas_call x1, Pallas kernels, per_device(): pl.pallas_call(functools.partial(kernel, peers), out_shape=(jax.ShapeDtyp...  39.9 us
    unnamed x3, local copies, waits for them, and re-layouts  4.64 us

profile of v3, /device:TPU:1, one launch (start us, length us, event | category | flops | bytes accessed | tf_op | source)
XLA Modules:
  0.0 45.2 jit_solution(317378307659638875)
XLA Ops:
  0.6 39.9 %shard_map.139 = (f32[5,16384]{1,0:T(8,128)}, f32[3,512]{1,0:T(4,128)}, f32[3,4096]{1,0:T(4,128)}) custom-call(f32[5,16384]{1,0:T(8,128)} %refs_0_.1, f32[5,16384]{1,0:T(8,128)} %refs_1_.1, bf16[5,5,7,16384]{3,2,1,0:T(8,128)(2,1)} %bitcast.6, s32[7,16384]{1,0:T(8,128)} %refs_3_.1, f32[128,128]{1,0:T(8,128)} %bitcast.7, s32[6,512]{1,0:T(8,128)} %refs_5_.1, ...), custom_call_target="tpu_custom_call" | custom-call | tf_op jit(solution)/shard_map/pallas_call | solution.py:585
  40.6 1.9 %copy.18 = f32[5,16384]{1,0:T(8,128)} copy(f32[5,16384]{1,0:T(8,128)} %get-tuple-element.6) | data formatting | bytes 655360
  42.4 1.3 %copy.19 = f32[3,512]{1,0:T(4,128)} copy(f32[3,512]{1,0:T(4,128)} %get-tuple-element.7) | data formatting | bytes 12288
  43.7 1.5 %copy.20 = f32[3,4096]{1,0:T(4,128)} copy(f32[3,4096]{1,0:T(4,128)} %get-tuple-element.8) | data formatting | bytes 98304

commit v4 on v3

--- a/solution.py
+++ b/solution.py
@@ -181,32 +181,54 @@
             table[c, quarter * 8 : quarter * 8 + 8, :] = total
 
 
+def window(cols, cells, q, j):
+    col = cols[:, lanes(q * 4 + j)]
+    shifted = col + 64 - q * 512
+    far = col - cells
+    far_at = (far >> 9) * 16 + (far & 511) - q * 16
+    inside = col < cells
+    where_at = jnp.where(inside, shifted, far_at) & (LANES - 1)
+    return where_at, jnp.where(inside, shifted >> 7, 5)
+
+
+def pick_local(c, where_at, chunk, table, q):
+    total = pick(table[q * 4, c : c + 1, :], where_at)
+    for k in range(1, 5):
+        got = pick(table[q * 4 + k, c : c + 1, :], where_at)
+        total = jnp.where(chunk == k, got, total)
+    return total
+
+
+def early_picks(cells, cols, table, picks):
+    def step(q, carry):
+        for j in range(4):
+            where_at, chunk = window(cols, cells, q, j)
+            for c in range(5):
+                picks[c, q * 4 + j, 0:7, :] = pick_local(c, where_at, chunk, table, q)
+        return carry
+
+    lax.fori_loop(0, EARLY, step, 0, unroll=6)
+
+
 def apply_system(fluid, base, jac, cols, dt, table, halo, sums, picks, residual, state):
     cells = fluid.shape[1]
     sums[...] = jnp.zeros(sums.shape, F32)
 
-    def step(q, carry):
-        where_at, chunk = [], []
+    def step(q, carry, early):
         for j in range(4):
-            col = cols[:, lanes(q * 4 + j)]
-            shifted = col + 64 - q * 512
-            far = col - cells
-            far_at = (far >> 9) * 16 + (far & 511) - q * 16
-            inside = col < cells
-            where_at.append(jnp.where(inside, shifted, far_at) & (LANES - 1))
-            chunk.append(jnp.where(inside, shifted >> 7, 5))
-        for j in range(4):
+            where_at, chunk = window(cols, cells, q, j)
+            block = q * 4 + j
+            at = lanes(block)
             picked = []
             for c in range(5):
-                total = pick(table[q * 4, c : c + 1, :], where_at[j])
-                for k in range(1, 5):
-                    got = pick(table[q * 4 + k, c : c + 1, :], where_at[j])
-                    total = jnp.where(chunk[j] == k, got, total)
-                got = pick(halo[c, pl.ds(q, 1), :], where_at[j])
-                picked.append(jnp.where(chunk[j] == 5, got, total))
-            at = lanes(q * 4 + j)
+                if early:
+                    total = picks[c, block, 0:7, :]
+                else:
+                    total = pick_local(c, where_at, chunk, table, q)
+                got = pick(halo[c, pl.ds(q, 1), :], where_at)
+                picked.append(jnp.where(chunk == 5, got, total))
             for c in range(5):
-                picks[c, q * 4 + j, 0:7, :] = picked[c]
+                picks[c, block, 0:7, :] = picked[c]
             for r in (0, 1, 4):
                 total = jac[r, 0, :, at].astype(F32) * picked[0]
                 for c in range(1, 5):
@@ -217,13 +239,13 @@
                 coupled = coupled + sums[j, pl.ds(b, 5, stride=8), :]
             left = base[:, at] - coupled
             residual[:, at] = left
-            block = q * 4 + j
             state[pl.ds(pl.multiple_of(block * 8, 8), 5), :] = (
                 fluid[:, at] + dt[pl.ds(block, 1), :] * left
             )
         return carry
 
-    lax.fori_loop(0, cells // 512, step, 0, unroll=APPLY_UNROLL)
+    lax.fori_loop(0, EARLY, functools.partial(step, early=True), 0, unroll=6)
+    lax.fori_loop(EARLY, cells // 512, functools.partial(step, early=False), 0, unroll=10)
 
 
 def apply_rest(base, jac, picks, sums, residual):
@@ -369,7 +391,7 @@
                 motion[c : c + 1, at : at + LANES] = out[s : s + 1, :]
 
 
-APPLY_UNROLL = 4
+EARLY = 12
 COMPACT_UNROLL = 16
 INPUTS = ("fluid", "base", "jac", "cols", "dt", "send", "fcell", "area", "weight", "route", "fnode", "comp")
 
@@ -391,8 +413,8 @@
         name: pltpu.make_async_copy(hbm[name], v[name], in_sems.at[i])
         for i, name in enumerate(INPUTS)
     }
-    for name in ("fluid", "send", "route", "fcell", "fnode", "weight", "area", "cols", "jac", "base", "dt", "comp"):
-        copies[name].start()
+    copies["fluid"].start()
+    copies["send"].start()
     barrier = pltpu.get_barrier_semaphore()
 
     def greet(r, carry):
@@ -402,6 +424,8 @@
         return carry
 
     lax.fori_loop(1, peers, greet, 0)
+    for name in ("route", "fnode", "weight", "area", "cols", "fcell", "jac", "base", "dt", "comp"):
+        copies[name].start()
     copies["send"].wait()
     copies["fluid"].wait()
     gather_sends(v["fluid"], v["send"], index, found, sends)
@@ -428,10 +452,12 @@
     compact_faces(
         peers, onehot, rank, v["fnode"], v["weight"], v["area"], face_at, slab, scale
     )
+    copies["cols"].wait()
+    early_picks(v["fluid"].shape[1], v["cols"], table, picks)
     for copy in halo_copies:
         copy.wait()
     halo_table(arrived, halo)
-    for name in ("cols", "jac", "base", "dt", "fcell"):
+    for name in ("jac", "base", "dt", "fcell"):
         copies[name].wait()
     apply_system(
         v["fluid"], v["base"], v["jac"], v["cols"], v["dt"], table, halo, sums, picks, residual, state
@@ -439,17 +465,18 @@
     cell_pressures(state, pressure)
     face_loads(pressure, v["fcell"], scale, loads)
 
-    def copy_of(source, target, send_sem, recv_sem, slots, to, group):
+    def copy_of(source, target, send_sem, recv_sem, height, slots, to, group):
+        rows = pl.ds(0, height)
         return pltpu.make_async_remote_copy(
-            src_ref=source.at[slots],
-            dst_ref=target.at[slots],
+            src_ref=source.at[slots, rows],
+            dst_ref=target.at[slots, rows],
             send_sem=send_sem,
             recv_sem=recv_sem.at[group],
             device_id={"dom": to},
             device_id_type=MESH,
         )
 
-    def send_group(source, target, send_sem, recv_sem, sign, group, amount):
+    def send_group(source, target, send_sem, recv_sem, height, sign, group, amount):
         for place in range(amount):
             dz, dy, dc = offset_of(group, place)
             to = (
@@ -457,14 +484,15 @@
                 + (((me >> 1) + sign * dy + 4) & 3) * 2
                 + ((me + dc) & 1)
             )
-            copy_of(source, target, send_sem, recv_sem, group * 8 + place, to, group).start()
-
-    def received(source, target, send_sem, recv_sem, group, amount):
+            slot = group * 8 + place
+            copy_of(source, target, send_sem, recv_sem, height, slot, to, group).start()
+
+    def received(source, target, send_sem, recv_sem, height, group, amount):
         slots = pl.ds(group * 8, amount)
-        copy_of(source, target, send_sem, recv_sem, slots, me ^ 1, group).wait_recv()
-
-    forth = (slab, got, load_send, load_recv)
-    back = (reply, answer, back_send, back_recv)
+        copy_of(source, target, send_sem, recv_sem, height, slots, me ^ 1, group).wait_recv()
+
+    forth = (slab, got, load_send, load_recv, 4)
+    back = (reply, answer, back_send, back_recv, 3)
 
     def send_loads(g, carry):
         fill_slabs(g, loads, face_at, slab)
@@ -511,8 +539,8 @@
 
     motions = lax.fori_loop(0, 7, take_replies, motions)
     store_motions(motions, v["weight"], motion)
-    for source, target, send_sem, recv_sem in (forth, back):
-        copy_of(source, target, send_sem, recv_sem, pl.ds(0, 63), me ^ 1, 0).wait_send()
+    for way in (forth, back):
+        copy_of(*way, pl.ds(0, 63), me ^ 1, 0).wait_send()
     residual_copy.wait()
 
 
@@ -582,7 +610,7 @@
         dma,
         dma((8,)),
     ]
-    return pl.pallas_call(
+    results = pl.pallas_call(
         functools.partial(kernel, peers),
         out_shape=(
             jax.ShapeDtypeStruct(fluid_state.shape, F32),
@@ -600,6 +628,27 @@
             collective_id=0, has_side_effects=True, vmem_limit_bytes=56 * 1024 * 1024
         ),
     )(*operands)
+    return hand_over(*results)
+
+
+def hand_over_kernel(*refs):
+    sems = refs[-1]
+    copies = [pltpu.make_async_copy(refs[i], refs[3 + i], sems.at[i]) for i in range(3)]
+    for copy in copies:
+        copy.start()
+    for copy in copies:
+        copy.wait()
+
+
+def hand_over(*results):
+    return pl.pallas_call(
+        hand_over_kernel,
+        out_shape=[jax.ShapeDtypeStruct(x.shape, x.dtype) for x in results],
+        in_specs=[pl.BlockSpec(memory_space=pl.ANY)] * 3,
+        out_specs=[pl.BlockSpec(memory_space=pl.ANY)] * 3,
+        scratch_shapes=[pltpu.SemaphoreType.DMA((3,))],
+        compiler_params=pltpu.CompilerParams(vmem_limit_bytes=60 * 1024 * 1024),
+    )(*results)
 
 
 def solution(mesh):

time: 45.4 us -> 59 us (1.30)
  Pallas kernels: 39.9 us -> 58.3 us
  local copies, waits for them, and re-layouts: 4.64 us -> 0 us
    pallas_call x0 -> x1, Pallas kernels: none -> 19.2 us  [hand_over(): pl.pallas_call(hand_over_kernel, out_shape=[jax.ShapeDtypeStruct(x.shape,...]
    unnamed x3 -> x0, local copies, waits for them, and re-layouts: 4.64 us -> none
    pallas_call x1, Pallas kernels: 39.9 us -> 39.1 us  [per_device(): pl.pallas_call(functools.partial(kernel, peers), out_shape=(jax.ShapeDtyp...]
where the time goes in v4:
time: 59 us
  Pallas kernels  58.3 us (99%)
  between operations  0.64 us (1%)
    pallas_call x1, Pallas kernels, per_device(): pl.pallas_call(functools.partial(kernel, peers), out_shape=(jax.ShapeDtyp...  39.1 us
    pallas_call x1, Pallas kernels, hand_over(): pl.pallas_call(hand_over_kernel, out_shape=[jax.ShapeDtypeStruct(x.shape,...  19.2 us

profile of v4, /device:TPU:1, one launch (start us, length us, event | category | flops | bytes accessed | tf_op | source)
XLA Modules:
  0.0 59.0 jit_solution(9284590450288063829)
XLA Ops:
  0.6 39.1 %shard_map.139 = (f32[5,16384]{1,0:T(8,128)}, f32[3,512]{1,0:T(4,128)}, f32[3,4096]{1,0:T(4,128)}) custom-call(f32[5,16384]{1,0:T(8,128)} %refs_0_.1, f32[5,16384]{1,0:T(8,128)} %refs_1_.1, bf16[5,5,7,16384]{3,2,1,0:T(8,128)(2,1)} %bitcast.6, s32[7,16384]{1,0:T(8,128)} %refs_3_.1, f32[128,128]{1,0:T(8,128)} %bitcast.7, s32[6,512]{1,0:T(8,128)} %refs_5_.1, ...), custom_call_target="tpu_custom_call" | custom-call | tf_op jit(solution)/shard_map/pallas_call | solution.py:613
  39.7 19.2 %shard_map.140 = (f32[5,16384]{1,0:T(8,128)}, f32[3,512]{1,0:T(4,128)}, f32[3,4096]{1,0:T(4,128)}) custom-call(f32[5,16384]{1,0:T(8,128)} %get-tuple-element.6.refs_0_, f32[3,512]{1,0:T(4,128)} %get-tuple-element.7.refs_1_, f32[3,4096]{1,0:T(4,128)} %get-tuple-element.8.refs_2_), custom_call_target="tpu_custom_call" | custom-call | tf_op jit(solution)/shard_map/pallas_call | solution.py:644

commit v5 on v4

--- a/solution.py
+++ b/solution.py
@@ -632,12 +632,30 @@
 
 
 def hand_over_kernel(*refs):
-    sems = refs[-1]
-    copies = [pltpu.make_async_copy(refs[i], refs[3 + i], sems.at[i]) for i in range(3)]
-    for copy in copies:
-        copy.start()
-    for copy in copies:
-        copy.wait()
+    sources, targets, holds, (sems_in, sems_out) = refs[:3], refs[3:6], refs[6:9], refs[9:]
+    pieces = []
+    for which, count in ((0, 4), (1, 1), (2, 1)):
+        width = sources[which].shape[1] // count
+        for piece in range(count):
+            at = (slice(None), pl.ds(piece * width, width))
+            n = len(pieces)
+            pieces.append(
+                (
+                    pltpu.make_async_copy(
+                        sources[which].at[at], holds[which].at[at], sems_in.at[n]
+                    ),
+                    pltpu.make_async_copy(
+                        holds[which].at[at], targets[which].at[at], sems_out.at[n]
+                    ),
+                )
+            )
+    for copy_in, _ in pieces:
+        copy_in.start()
+    for copy_in, copy_out in pieces:
+        copy_in.wait()
+        copy_out.start()
+    for _, copy_out in pieces:
+        copy_out.wait()
 
 
 def hand_over(*results):
@@ -646,7 +664,8 @@
         out_shape=[jax.ShapeDtypeStruct(x.shape, x.dtype) for x in results],
         in_specs=[pl.BlockSpec(memory_space=pl.ANY)] * 3,
         out_specs=[pl.BlockSpec(memory_space=pl.ANY)] * 3,
-        scratch_shapes=[pltpu.SemaphoreType.DMA((3,))],
+        scratch_shapes=[pltpu.VMEM(x.shape, x.dtype) for x in results]
+        + [pltpu.SemaphoreType.DMA((6,))] * 2,
         compiler_params=pltpu.CompilerParams(vmem_limit_bytes=60 * 1024 * 1024),
     )(*results)
 

time: 59 us -> 41.7 us (0.71)
  Pallas kernels: 58.3 us -> 40.9 us
    pallas_call x1, Pallas kernels: 19.2 us -> 1.88 us  [hand_over(): pl.pallas_call(hand_over_kernel, out_shape=[jax.ShapeDtypeStruct(x.shape,...]
where the time goes in v5:
time: 41.7 us; the launch traced here: 41.6 us
  Pallas kernels  40.9 us (98%)
  between operations  0.64 us (2%)
    pallas_call x1, Pallas kernels, per_device(): pl.pallas_call(functools.partial(kernel, peers), out_shape=(jax.ShapeDtyp...  39.1 us
    pallas_call x1, Pallas kernels, hand_over(): pl.pallas_call(hand_over_kernel, out_shape=[jax.ShapeDtypeStruct(x.shape,...  1.88 us

profile of v5, /device:TPU:1, one launch (start us, length us, event | category | flops | bytes accessed | tf_op | source)
XLA Modules:
  0.0 41.6 jit_solution(10490516372386908501)
XLA Ops:
  0.6 39.1 %shard_map.139 = (f32[5,16384]{1,0:T(8,128)}, f32[3,512]{1,0:T(4,128)}, f32[3,4096]{1,0:T(4,128)}) custom-call(f32[5,16384]{1,0:T(8,128)} %refs_0_.1, f32[5,16384]{1,0:T(8,128)} %refs_1_.1, bf16[5,5,7,16384]{3,2,1,0:T(8,128)(2,1)} %bitcast.6, s32[7,16384]{1,0:T(8,128)} %refs_3_.1, f32[128,128]{1,0:T(8,128)} %bitcast.7, s32[6,512]{1,0:T(8,128)} %refs_5_.1, ...), custom_call_target="tpu_custom_call" | custom-call | tf_op jit(solution)/shard_map/pallas_call | solution.py:613
  39.7 1.9 %shard_map.140 = (f32[5,16384]{1,0:T(8,128)}, f32[3,512]{1,0:T(4,128)}, f32[3,4096]{1,0:T(4,128)}) custom-call(f32[5,16384]{1,0:T(8,128)} %get-tuple-element.6.refs_0_, f32[3,512]{1,0:T(4,128)} %get-tuple-element.7.refs_1_, f32[3,4096]{1,0:T(4,128)} %get-tuple-element.8.refs_2_), custom_call_target="tpu_custom_call" | custom-call | tf_op jit(solution)/shard_map/pallas_call | solution.py:662

commit v6 on v5

--- a/solution.py
+++ b/solution.py
@@ -292,7 +292,7 @@
             loads[rows, :] = scale[rows, :] * found
         return carry
 
-    lax.fori_loop(0, 4, part, 0)
+    lax.fori_loop(0, 4, part, 0, unroll=2)
 
 
 def fill_slabs(g, loads, face_at, slab):
@@ -311,23 +311,26 @@
         slab[rows, c, :] = total[c]
 
 
-def node_sums(g, got):
+def node_sums(groups, got):
     line = iota((LANES, LANES), 0)
     above = iota((8, LANES), 0) >> 2
-    left, right = [], []
-    for s in range(8):
-        piece = got[g * 8 + s]
-        node = piece[3:4, :].astype(I32)
-        twice = jnp.concatenate([piece, piece], axis=0)
-        high = jnp.broadcast_to(node >> 7, (8, LANES))
-        spread = jnp.concatenate(
-            [jnp.where(high == above, twice, 0.0), jnp.where(high == above + 2, twice, 0.0)],
-            axis=0,
-        )
-        left.append(jnp.concatenate(three_parts(spread), axis=0))
-        hit = jnp.broadcast_to(node & (LANES - 1), (LANES, LANES)) == line
-        right.append(jnp.where(hit, 1.0, 0.0).astype(BF16))
-    return dot_nt(jnp.concatenate(left, axis=1), jnp.concatenate(right, axis=1))
+    total = jnp.zeros((48, LANES), F32)
+    for g in groups:
+        left, right = [], []
+        for s in range(8):
+            piece = got[g * 8 + s]
+            node = piece[3:4, :].astype(I32)
+            twice = jnp.concatenate([piece, piece], axis=0)
+            high = jnp.broadcast_to(node >> 7, (8, LANES))
+            spread = jnp.concatenate(
+                [jnp.where(high == above, twice, 0.0), jnp.where(high == above + 2, twice, 0.0)],
+                axis=0,
+            )
+            left.append(jnp.concatenate(three_parts(spread), axis=0))
+            hit = jnp.broadcast_to(node & (LANES - 1), (LANES, LANES)) == line
+            right.append(jnp.where(hit, 1.0, 0.0).astype(BF16))
+        total = total + dot_nt(jnp.concatenate(left, axis=1), jnp.concatenate(right, axis=1))
+    return total
 
 
 def split_compliance(compliance, high, middle):
@@ -346,12 +349,14 @@
     sums = total[0:16, :] + total[16:32, :] + total[32:48, :]
     for t in range(4):
         load = jnp.concatenate([sums[t * 4 + c : t * 4 + c + 1, :] for c in range(3)], axis=1)
-        parts = jnp.concatenate(
-            [jnp.broadcast_to(part, (16, part.shape[1])) for part in three_parts(load)], axis=0
+        top, rest, last = (
+            jnp.broadcast_to(part.astype(F32), (16, part.shape[1])) for part in three_parts(load)
         )
+        line = iota(top.shape, 0)
+        parts = jnp.where(line == 0, top, jnp.where(line == 1, rest, last)).astype(BF16)
         first = dot_nt(parts, high[t])
-        second = dot_nt(parts[0:32], middle[t])
-        out = first[0:1] + ((first[16:17] + second[0:1]) + (first[32:33] + second[16:17]))
+        second = dot_nt(parts, middle[t])
+        out = first[0:1] + ((first[1:2] + second[0:1]) + (first[2:3] + second[1:2]))
         for c in range(3):
             row = out[:, c * LANES : (c + 1) * LANES]
             moved[c * 4 + t : c * 4 + t + 1, :] = row
@@ -369,16 +374,17 @@
         reply[rows, c, :] = total
 
 
-def face_motions(g, total, answer, relative, rank):
+def face_motions(groups, total, answer, relative, rank):
     total = list(total)
     for f in range(4):
         rows = slice(f * 8, f * 8 + 8)
         slot, peer = rank[rows, :].astype(I32), relative[rows, :]
-        for s in range(8):
-            hit = peer == g * 8 + s
-            for c in range(3):
-                row = answer[g * 8 + s, c : c + 1, :]
-                total[c * 4 + f] = jnp.where(hit, pick(row, slot), total[c * 4 + f])
+        for g in groups:
+            for s in range(8):
+                hit = peer == g * 8 + s
+                for c in range(3):
+                    row = answer[g * 8 + s, c : c + 1, :]
+                    total[c * 4 + f] = jnp.where(hit, pick(row, slot), total[c * 4 + f])
     return tuple(total)
 
 
@@ -392,6 +398,7 @@
 
 
 EARLY = 12
+BATCHES = ((7, 6, 5, 4), (3, 2, 1, 0))
 COMPACT_UNROLL = 16
 INPUTS = ("fluid", "base", "jac", "cols", "dt", "send", "fcell", "area", "weight", "route", "fnode", "comp")
 
@@ -417,13 +424,19 @@
     copies["send"].start()
     barrier = pltpu.get_barrier_semaphore()
 
-    def greet(r, carry):
+
+    def peer_at(slot, sign):
+        dz, dy, dc = offset_of(slot // 8, slot % 8)
+        return (
+            (((me >> 3) + sign * dz + 8) & 7) * 8
+            + (((me >> 1) + sign * dy + 4) & 3) * 2
+            + ((me + dc) & 1)
+        )
+
+    for slot in range(peers - 1):
         pl.semaphore_signal(
-            barrier, inc=1, device_id={"dom": (me + r) & (peers - 1)}, device_id_type=MESH
+            barrier, inc=1, device_id={"dom": peer_at(slot, 1)}, device_id_type=MESH
         )
-        return carry
-
-    lax.fori_loop(1, peers, greet, 0)
     for name in ("route", "fnode", "weight", "area", "cols", "fcell", "jac", "base", "dt", "comp"):
         copies[name].start()
     copies["send"].wait()
@@ -478,13 +491,8 @@
 
     def send_group(source, target, send_sem, recv_sem, height, sign, group, amount):
         for place in range(amount):
-            dz, dy, dc = offset_of(group, place)
-            to = (
-                (((me >> 3) + sign * dz + 8) & 7) * 8
-                + (((me >> 1) + sign * dy + 4) & 3) * 2
-                + ((me + dc) & 1)
-            )
             slot = group * 8 + place
+            to = peer_at(slot, sign)
             copy_of(source, target, send_sem, recv_sem, height, slot, to, group).start()
 
     def received(source, target, send_sem, recv_sem, height, group, amount):
@@ -510,14 +518,11 @@
     copies["comp"].wait()
     split_compliance(v["comp"], comp_high, comp_middle)
 
-    received(*forth, 7, 7)
-    total = node_sums(7, got)
-
-    def take_loads(i, total):
-        received(*forth, 6 - i, 8)
-        return total + node_sums(6 - i, got)
-
-    total = lax.fori_loop(0, 7, take_loads, total)
+    total = jnp.zeros((48, LANES), F32)
+    for groups in BATCHES:
+        for g in groups:
+            received(*forth, g, 8 if g < 7 else 7)
+        total = total + node_sums(groups, got)
     tile_response(total, comp_high, comp_middle, moved, displacement)
 
     def send_replies(g, carry):
@@ -530,14 +535,11 @@
     send_group(*back, -1, 7, 7)
     answer[63] = reply[63]
 
-    received(*back, 7, 7)
-    motions = face_motions(7, (jnp.zeros((8, LANES), F32),) * 12, answer, relative, rank)
-
-    def take_replies(i, total):
-        received(*back, 6 - i, 8)
-        return face_motions(6 - i, total, answer, relative, rank)
-
-    motions = lax.fori_loop(0, 7, take_replies, motions)
+    motions = (jnp.zeros((8, LANES), F32),) * 12
+    for groups in BATCHES:
+        for g in groups:
+            received(*back, g, 8 if g < 7 else 7)
+        motions = face_motions(groups, motions, answer, relative, rank)
     store_motions(motions, v["weight"], motion)
     for way in (forth, back):
         copy_of(*way, pl.ds(0, 63), me ^ 1, 0).wait_send()

time: 41.7 us -> 41.3 us (level)
  no operation moved by 1% of the time
where the time goes in v6:
time: 41.3 us; the launch traced here: 41.2 us
  Pallas kernels  40.6 us (98%)
  between operations  0.64 us (2%)
    pallas_call x1, Pallas kernels, per_device(): pl.pallas_call(functools.partial(kernel, peers), out_shape=(jax.ShapeDtyp...  38.7 us
    pallas_call x1, Pallas kernels, hand_over(): pl.pallas_call(hand_over_kernel, out_shape=[jax.ShapeDtypeStruct(x.shape,...  1.88 us

profile of v6, /device:TPU:1, one launch (start us, length us, event | category | flops | bytes accessed | tf_op | source)
XLA Modules:
  0.0 41.2 jit_solution(12425794616448733018)
XLA Ops:
  0.6 38.7 %shard_map.139 = (f32[5,16384]{1,0:T(8,128)}, f32[3,512]{1,0:T(4,128)}, f32[3,4096]{1,0:T(4,128)}) custom-call(f32[5,16384]{1,0:T(8,128)} %refs_0_.1, f32[5,16384]{1,0:T(8,128)} %refs_1_.1, bf16[5,5,7,16384]{3,2,1,0:T(8,128)(2,1)} %bitcast.6, s32[7,16384]{1,0:T(8,128)} %refs_3_.1, f32[128,128]{1,0:T(8,128)} %bitcast.7, s32[6,512]{1,0:T(8,128)} %refs_5_.1, ...), custom_call_target="tpu_custom_call" | custom-call | tf_op jit(solution)/shard_map/pallas_call | solution.py:615
  39.3 1.9 %shard_map.140 = (f32[5,16384]{1,0:T(8,128)}, f32[3,512]{1,0:T(4,128)}, f32[3,4096]{1,0:T(4,128)}) custom-call(f32[5,16384]{1,0:T(8,128)} %get-tuple-element.6.refs_0_, f32[3,512]{1,0:T(4,128)} %get-tuple-element.7.refs_1_, f32[3,4096]{1,0:T(4,128)} %get-tuple-element.8.refs_2_), custom_call_target="tpu_custom_call" | custom-call | tf_op jit(solution)/shard_map/pallas_call | solution.py:664

commit v7 on v6

--- a/solution.py
+++ b/solution.py
@@ -113,7 +113,7 @@
         prefix[rows, :] = jnp.dot(onehot[rows, :], weights, preferred_element_type=F32)
         return carry
 
-    lax.fori_loop(0, 32 * peers // 512, count, 0)
+    lax.fori_loop(0, 32 * peers // 512, count, 0, unroll=4)
 
     def step(i, before):
         rows = pl.ds(pl.multiple_of(i * peers, peers), peers)
@@ -122,7 +122,7 @@
         rank[pl.ds(i, 1), :] = jnp.sum(hit * here, axis=0, keepdims=True) - 1.0
         return before + prefix[rows, LANES : 2 * LANES]
 
-    lax.fori_loop(0, 32, step, jnp.zeros((peers, LANES), F32), unroll=2)
+    lax.fori_loop(0, 32, step, jnp.zeros((peers, LANES), F32), unroll=16)
 
 
 def compact_faces(peers, onehot, rank, fnode, weight, area, face_at, slab, scale):
@@ -245,7 +245,7 @@
         return carry
 
     lax.fori_loop(0, EARLY, functools.partial(step, early=True), 0, unroll=6)
-    lax.fori_loop(EARLY, cells // 512, functools.partial(step, early=False), 0, unroll=10)
+    lax.fori_loop(EARLY, cells // 512, functools.partial(step, early=False), 0, unroll=7)
 
 
 def apply_rest(base, jac, picks, sums, residual):
@@ -397,7 +397,7 @@
                 motion[c : c + 1, at : at + LANES] = out[s : s + 1, :]
 
 
-EARLY = 12
+EARLY = 18
 BATCHES = ((7, 6, 5, 4), (3, 2, 1, 0))
 COMPACT_UNROLL = 16
 INPUTS = ("fluid", "base", "jac", "cols", "dt", "send", "fcell", "area", "weight", "route", "fnode", "comp")

time: 41.3 us -> 41 us (level)
  no operation moved by 1% of the time
where the time goes in v7:
time: 41 us; the launch traced here: 40.9 us
  Pallas kernels  40.2 us (98%)
  between operations  0.64 us (2%)
    pallas_call x1, Pallas kernels, per_device(): pl.pallas_call(functools.partial(kernel, peers), out_shape=(jax.ShapeDtyp...  38.4 us
    pallas_call x1, Pallas kernels, hand_over(): pl.pallas_call(hand_over_kernel, out_shape=[jax.ShapeDtypeStruct(x.shape,...  1.88 us

profile of v7, /device:TPU:1, one launch (start us, length us, event | category | flops | bytes accessed | tf_op | source)
XLA Modules:
  0.0 40.9 jit_solution(8737182393227782935)
XLA Ops:
  0.6 38.4 %shard_map.139 = (f32[5,16384]{1,0:T(8,128)}, f32[3,512]{1,0:T(4,128)}, f32[3,4096]{1,0:T(4,128)}) custom-call(f32[5,16384]{1,0:T(8,128)} %refs_0_.1, f32[5,16384]{1,0:T(8,128)} %refs_1_.1, bf16[5,5,7,16384]{3,2,1,0:T(8,128)(2,1)} %bitcast.6, s32[7,16384]{1,0:T(8,128)} %refs_3_.1, f32[128,128]{1,0:T(8,128)} %bitcast.7, s32[6,512]{1,0:T(8,128)} %refs_5_.1, ...), custom_call_target="tpu_custom_call" | custom-call | tf_op jit(solution)/shard_map/pallas_call | solution.py:615
  39.0 1.9 %shard_map.140 = (f32[5,16384]{1,0:T(8,128)}, f32[3,512]{1,0:T(4,128)}, f32[3,4096]{1,0:T(4,128)}) custom-call(f32[5,16384]{1,0:T(8,128)} %get-tuple-element.6.refs_0_, f32[3,512]{1,0:T(4,128)} %get-tuple-element.7.refs_1_, f32[3,4096]{1,0:T(4,128)} %get-tuple-element.8.refs_2_), custom_call_target="tpu_custom_call" | custom-call | tf_op jit(solution)/shard_map/pallas_call | solution.py:664

commit v8 on v7

--- a/solution.py
+++ b/solution.py
@@ -60,11 +60,12 @@
     return group * 8 + side * 2 + (1 - dc)
 
 
-def gather_sends(fluid, send, index, found, out):
+def gather_sends(fluid, send, index, found, out, beside=lambda g: None):
     for k in range(4):
         index[pl.ds(k, 6, stride=4), :] = send[:, k * LANES : (k + 1) * LANES]
 
     def part(g, carry):
+        beside(g)
         rows = pl.ds(pl.multiple_of(g * 8, 8), 8)
         cell = index[rows, :]
         low, high = cell & (LANES - 1), cell >> 7
@@ -433,15 +434,22 @@
             + ((me + dc) & 1)
         )
 
-    for slot in range(peers - 1):
+    def greet(slot):
         pl.semaphore_signal(
             barrier, inc=1, device_id={"dom": peer_at(slot, 1)}, device_id_type=MESH
         )
+
+    def greet_near(g):
+        for place in range(9):
+            greet(36 + g * 9 + place)
+
+    for slot in range(36):
+        greet(slot)
     for name in ("route", "fnode", "weight", "area", "cols", "fcell", "jac", "base", "dt", "comp"):
         copies[name].start()
     copies["send"].wait()
     copies["fluid"].wait()
-    gather_sends(v["fluid"], v["send"], index, found, sends)
+    gather_sends(v["fluid"], v["send"], index, found, sends, greet_near)
     pl.semaphore_wait(barrier, peers - 1)
 
     halo_copies = []

time: 41 us -> 41 us (level)
  no operation moved by 1% of the time
where the time goes in v8:
time: 41 us; the launch traced here: 40.9 us
  Pallas kernels  40.3 us (98%)
  between operations  0.64 us (2%)
    pallas_call x1, Pallas kernels, per_device(): pl.pallas_call(functools.partial(kernel, peers), out_shape=(jax.ShapeDtyp...  38.4 us
    pallas_call x1, Pallas kernels, hand_over(): pl.pallas_call(hand_over_kernel, out_shape=[jax.ShapeDtypeStruct(x.shape,...  1.88 us

profile of v8, /device:TPU:1, one launch (start us, length us, event | category | flops | bytes accessed | tf_op | source)
XLA Modules:
  0.0 40.9 jit_solution(16086766749230770189)
XLA Ops:
  0.6 38.4 %shard_map.139 = (f32[5,16384]{1,0:T(8,128)}, f32[3,512]{1,0:T(4,128)}, f32[3,4096]{1,0:T(4,128)}) custom-call(f32[5,16384]{1,0:T(8,128)} %refs_0_.1, f32[5,16384]{1,0:T(8,128)} %refs_1_.1, bf16[5,5,7,16384]{3,2,1,0:T(8,128)(2,1)} %bitcast.6, s32[7,16384]{1,0:T(8,128)} %refs_3_.1, f32[128,128]{1,0:T(8,128)} %bitcast.7, s32[6,512]{1,0:T(8,128)} %refs_5_.1, ...), custom_call_target="tpu_custom_call" | custom-call | tf_op jit(solution)/shard_map/pallas_call | solution.py:623
  39.1 1.9 %shard_map.140 = (f32[5,16384]{1,0:T(8,128)}, f32[3,512]{1,0:T(4,128)}, f32[3,4096]{1,0:T(4,128)}) custom-call(f32[5,16384]{1,0:T(8,128)} %get-tuple-element.6.refs_0_, f32[3,512]{1,0:T(4,128)} %get-tuple-element.7.refs_1_, f32[3,4096]{1,0:T(4,128)} %get-tuple-element.8.refs_2_), custom_call_target="tpu_custom_call" | custom-call | tf_op jit(solution)/shard_map/pallas_call | solution.py:672
